TPU v7x, 256 devices: a whole 4x4x8 slice. The times are simulated.
256 devices in a mesh: view: 2 (over core), dom: 128 (over y, x, z).
Axes of the slice: x: 4, y: 4, z: 8, core: 2. Of those that a mesh axis runs over, the one named last changes fastest.
Arguments:
- features: bfloat16 [2, 131072, 256], P('view', 'dom'), may hold values from -6 to 6
- local_adjacency: bfloat16 [2, 131072, 1024], P('view', 'dom'), may hold values from -0.1875 to 0.1875
- tile_keep: int32 [2, 1024, 8], P('view', 'dom'), may hold values 0 or 1
- halo_adjacency: bfloat16 [2, 131072, 1024], P('view', 'dom'), may hold values from -0.1875 to 0.1875
- send_rows: int32 [2, 16384, 8], P('view', 'dom'), may hold values from 0 to 1023
- send_count: int32 [2, 16384], P('view', 'dom'), may hold values from 1 to 8, as said below
- target: bfloat16 [2, 131072, 256], P('view', 'dom'), may hold values from -6 to 6
- w_encoder: bfloat16 [256, 256], replicated, may hold values from -0.375 to 0.375
- b_encoder: float32 [256], replicated, may hold values from -3 to 3
- w_predict_in: bfloat16 [256, 512], replicated, may hold values from -0.375 to 0.375
- b_predict_in: float32 [512], replicated, may hold values from -3 to 3
- w_predict_out: bfloat16 [512, 256], replicated, may hold values from -0.25 to 0.25
Outputs:
- features_grad: bfloat16 [2, 131072, 256], P('view', 'dom')
- encoder_w_grad: float32 [256, 256], replicated
- encoder_b_grad: float32 [256], replicated
- predict_in_w_grad: float32 [256, 512], replicated
- predict_in_b_grad: float32 [512], replicated
- predict_out_w_grad: float32 [512, 256], replicated
Inputs may be any that keep to these rules, and one draw needn't show every extreme that they name: `send_count`: some pairs of partitions fill all 8 slots in every draw.
All inputs are finite; a program needn't handle non-finite values. No bound on the sum of `tile_keep` on one device may be relied on, other than what follows from the above.
Results may differ from a plain program's by a relative error of at most 0.012.
Values may be sent and summed in bfloat16 or wider, within the bound.
A program may use at most 64 MiB of HBM per device.

v0:
```python
import jax
import jax.numpy as jnp
from jax import lax
from jax.sharding import PartitionSpec as P

loss_scale = 64.0


def swapped(value, axis, apart):
    mask = 2**apart
    pairs = [(source, source ^ mask) for source in range(lax.axis_size(axis))]
    return lax.ppermute(value, axis, pairs)


def partition_pass(
    own_rows,
    adjacency,
    keep_tiles,
    halo_weights,
    received,
    other_target,
    w_encoder,
    b_encoder,
    w_predict_in,
    b_predict_in,
    w_predict_out,
):
    blocks = adjacency.shape[0] // 128
    kept = (
        adjacency.reshape(blocks, 128, blocks, 128)
        * keep_tiles.astype(adjacency.dtype)[:, None, :, None]
    ).reshape(adjacency.shape)
    flat_received = received.reshape(-1, own_rows.shape[1])
    aggregated = (
        jnp.dot(kept, own_rows, preferred_element_type=jnp.float32)
        + jnp.dot(halo_weights, flat_received, preferred_element_type=jnp.float32)
    ).astype(jnp.bfloat16)
    pre_encoder = jnp.dot(aggregated, w_encoder, preferred_element_type=jnp.float32) + b_encoder
    embed_value, embed_back = jax.vjp(jax.nn.gelu, pre_encoder)
    embedding = embed_value.astype(jnp.bfloat16)
    pre_hidden = jnp.dot(embedding, w_predict_in, preferred_element_type=jnp.float32) + b_predict_in
    hidden_value, hidden_back = jax.vjp(jax.nn.gelu, pre_hidden)
    hidden = hidden_value.astype(jnp.bfloat16)
    prediction = jnp.dot(hidden, w_predict_out, preferred_element_type=jnp.float32)
    target_value = other_target.astype(jnp.float32)
    squares_p = jnp.sum(prediction * prediction, axis=1, keepdims=True) + 1e-06
    squares_t = jnp.sum(target_value * target_value, axis=1, keepdims=True) + 1e-06
    joint = jnp.sqrt(squares_p * squares_t)
    cosine = jnp.sum(prediction * target_value, axis=1, keepdims=True) / joint
    prediction_grad = (
        -2.0 * loss_scale * (target_value / joint - cosine * prediction / squares_p)
    ).astype(jnp.bfloat16)
    grad_out = jnp.dot(hidden.T, prediction_grad, preferred_element_type=jnp.float32)
    hidden_grad = hidden_back(
        jnp.dot(prediction_grad, w_predict_out.T, preferred_element_type=jnp.float32)
    )[0].astype(jnp.bfloat16)
    grad_in_bias = jnp.sum(hidden_grad.astype(jnp.float32), axis=0)
    grad_in = jnp.dot(embedding.T, hidden_grad, preferred_element_type=jnp.float32)
    embedding_grad = embed_back(
        jnp.dot(hidden_grad, w_predict_in.T, preferred_element_type=jnp.float32)
    )[0].astype(jnp.bfloat16)
    grad_enc_bias = jnp.sum(embedding_grad.astype(jnp.float32), axis=0)
    grad_enc = jnp.dot(aggregated.T, embedding_grad, preferred_element_type=jnp.float32)
    aggregated_grad = jnp.dot(
        embedding_grad, w_encoder.T, preferred_element_type=jnp.float32
    ).astype(jnp.bfloat16)
    local_grad = jnp.dot(kept.T, aggregated_grad, preferred_element_type=jnp.float32)
    received_grad = (
        jnp.dot(halo_weights.T, aggregated_grad, preferred_element_type=jnp.float32)
        .astype(jnp.bfloat16)
        .reshape(received.shape)
    )
    return (local_grad, received_grad, (grad_enc, grad_enc_bias, grad_in, grad_in_bias, grad_out))


def local(
    features,
    local_adjacency,
    tile_keep,
    halo_adjacency,
    send_rows,
    send_count,
    target,
    w_encoder,
    b_encoder,
    w_predict_in,
    b_predict_in,
    w_predict_out,
):
    own_rows = features[0]
    node_count = own_rows.shape[0]
    width = own_rows.shape[1]
    row_table = send_rows[0]
    peers = row_table.shape[0]
    slots = row_table.shape[1]
    other_target = swapped(target, "view", 0)[0]
    live = jnp.arange(slots, dtype=jnp.int32)[None, :] < send_count[0][:, None]
    outgoing = jnp.where(
        live[:, :, None], jnp.take(own_rows, row_table, axis=0), jnp.zeros((), own_rows.dtype)
    )
    received = lax.all_to_all(outgoing, "dom", split_axis=0, concat_axis=0, tiled=True)
    local_grad, received_grad, grads = partition_pass(
        own_rows,
        local_adjacency[0],
        tile_keep[0],
        halo_adjacency[0],
        received,
        other_target,
        w_encoder,
        b_encoder,
        w_predict_in,
        b_predict_in,
        w_predict_out,
    )
    returned = lax.all_to_all(received_grad, "dom", split_axis=0, concat_axis=0, tiled=True)
    selector = (
        jnp.arange(node_count, dtype=jnp.int32)[:, None] == row_table.reshape(-1)[None, :]
    ) & live.reshape(-1)[None, :]
    feature_grad = local_grad + jnp.dot(
        selector.astype(jnp.bfloat16),
        returned.reshape(peers * slots, width),
        preferred_element_type=jnp.float32,
    )
    grads = lax.psum((grads[0], grads[1], grads[2], grads[3], grads[4]), ("view", "dom"))
    factor = 1.0 / jnp.sqrt(jnp.float32(2 * node_count * lax.axis_size("dom")))
    grad_enc, grad_enc_bias, grad_in, grad_in_bias, grad_out = tuple(
        (item * factor for item in grads)
    )
    return (
        feature_grad.astype(jnp.bfloat16)[None],
        grad_enc,
        grad_enc_bias,
        grad_in,
        grad_in_bias,
        grad_out,
    )


def solution(mesh):
    return jax.shard_map(
        local,
        mesh=mesh,
        in_specs=(
            P("view", "dom", None),
            P("view", "dom", None),
            P("view", "dom", None),
            P("view", "dom", None),
            P("view", "dom", None),
            P("view", "dom"),
            P("view", "dom", None),
            P(),
            P(),
            P(),
            P(),
            P(),
        ),
        out_specs=(P("view", "dom", None), P(), P(), P(), P(), P()),
        check_vma=False,
    )
```

profile of v0, /device:TPU:1, one launch (start us, length us, event | category | flops | bytes accessed | tf_op | source)
XLA Modules:
  0.0 337.9 jit_solution(354601421493320722)
XLA Ops:
  7.2 0.0 copy-start
  7.2 0.8 compare_and_fusion
  8.0 0.7 compare_select_fusion
  8.7 0.1 copy.22
  8.8 0.7 iota_compare_fusion.1
  9.6 0.1 copy.23
  9.7 0.1 reshape.138
  9.8 4.6 %gather_fusion = bf16[1024,256]{1,0:T(8,128)(2,1)S(1)} fusion(bf16[1024,256]{1,0:T(8,128)(2,1)} %bitcast.84, s32[1024]{0:T(1024)S(1)} %broadcast_clamp_fusion), kind=kCustom, calls=%fused_computation | custom fusion | bytes 1052672 | tf_op jit(solution)/shard_map/jit(_take)/gather | solution.py:99
  14.4 0.0 copy-start.5
  14.4 0.0 copy-start.6
  14.4 0.0 copy-start.7
  14.4 1.1 fusion.60
  15.5 16.9 %all-to-all-start = ((bf16[128,8,256]{2,1,0:T(8,128)(2,1)}), bf16[128,8,256]{2,1,0:T(8,128)(2,1)}, u32[]{:S(2)}, u32[]{:S(2)}) async-start(bf16[128,8,256]{2,1,0:T(8,128)(2,1)} %fusion.60), calls=%async_computation | async-start | bytes 1048576 | tf_op jit(solution)/shard_map/all_to_all | solution.py:101
  32.4 0.0 all-reduce.4.cloned.1.call-start
  32.5 0.0 copy-done.5
  32.5 1.0 copy.21
  33.5 1.0 collective-permute-start
  34.4 0.1 lt.55
  34.5 0.0 copy-done.6
  34.5 0.1 copy.25
  34.6 0.1 eq.16
  34.7 0.0 copy-done.7
  34.8 1.7 mul.170
  36.5 4.1 %mul.173 = bf16[1,1024,1024]{2,1,0:T(8,128)(2,1)} reshape(bf16[8,128,8,128]{3,2,1,0:T(8,128)(2,1)} %mul.170) | data formatting | bytes 4194304 | tf_op jit(solution)/shard_map/mul | solution.py:30
  40.6 0.0 copy-start.1
  40.6 10.5 %all-to-all-done = bf16[128,8,256]{2,1,0:T(8,128)(2,1)} async-done(((bf16[128,8,256]{2,1,0:T(8,128)(2,1)}), bf16[128,8,256]{2,1,0:T(8,128)(2,1)}, u32[]{:S(2)}, u32[]{:S(2)}) %all-to-all-start) | async-done | bytes 524320 | tf_op jit(solution)/shard_map/all_to_all | solution.py:101
  51.1 0.0 copy-done
  51.1 0.0 copy-start.2
  51.1 1.9 fusion.22
  53.0 0.0 copy-done.1
  53.0 0.0 copy-done.2
  53.0 0.4 copy-done.3
  53.5 0.7 fusion.37
  54.2 0.2 copy-done.4
  54.4 0.0 copy-done.8
  54.4 0.3 convolution_add_fusion
  54.7 0.0 copy-done.10
  54.7 0.0 copy-done.11
  54.7 0.0 copy-start.9
  54.7 1.1 multiply_convert_fusion
  55.8 0.0 collective-permute-done
  55.8 0.0 copy-done.9
  55.9 0.6 fusion.57
  56.5 0.3 fusion.56
  56.7 1.3 fusion.67
  58.0 1.8 convert_reduce_fusion
  59.8 1.4 fusion.63
  61.2 1.0 convert_reduce_fusion.1
  62.1 1.0 fusion.66
  63.2 0.3 convolution_convert_fusion
  63.5 4.2 %fusion.10 = f32[1024,256]{1,0:T(8,128)} fusion(bf16[1024,256]{1,0:T(8,128)(2,1)S(1)} %convolution_convert_fusion, bf16[128,8,8,128]{3,2,1,0:T(8,128)(2,1)} %bitcast.85, bf16[1,1024,1024]{2,1,0:T(8,128)(2,1)} %param.13), kind=kOutput, calls=%fused_computation.14 | convolution fusion | flops 537919488 | bytes 5767168 | tf_op jit(solution)/shard_map/dot_general | solution.py:67
  67.7 0.0 all-reduce.4.cloned.1.call-update
  67.7 0.7 fusion.40
  68.4 1.0 copy.26
  69.4 6.4 %all-to-all-start.1 = ((bf16[128,8,256]{2,1,0:T(8,128)(2,1)}), bf16[128,8,256]{2,1,0:T(8,128)(2,1)S(1)}, u32[]{:S(2)}, u32[]{:S(2)}) async-start(bf16[128,8,256]{2,1,0:T(8,128)(2,1)} %bitcast.14), calls=%async_computation.1 | async-start | bytes 1048576 | tf_op jit(solution)/shard_map/all_to_all | solution.py:115
  75.8 78.4 %all-reduce = (f32[256]{0:T(256)S(1)}, f32[512]{0:T(512)S(1)}) all-reduce(f32[256]{0:T(256)S(1)} %get-tuple-element.14, f32[512]{0:T(512)S(1)} %get-tuple-element.22), channel_id=1, replica_groups=mesh['view'=2,'dom'=128] {'view','dom'}, use_global_device_ids=true, to_apply=%region_5.6 | all-reduce | flops 768 | bytes 6144 | tf_op jit(solution)/shard_map/psum | solution.py:124
  154.2 0.6 broadcast_multiply_fusion.4
  154.7 0.6 broadcast_multiply_fusion.3
  155.3 167.4 %all-reduce.4.cloned.1.call-done = (f32[256,256]{1,0:T(8,128)}, f32[256,512]{1,0:T(8,128)}, f32[512,256]{1,0:T(8,128)}) async-done(((f32[256,256]{1,0:T(8,128)}, f32[256,512]{1,0:T(8,128)}, f32[512,256]{1,0:T(8,128)}), (f32[256,256]{1,0:T(8,128)}, f32[256,512]{1,0:T(8,128)}, f32[512,256]{1,0:T(8,128)})) %all-reduce.4.cloned.1.call-update) | async-done | bytes 1310736 | tf_op jit(solution)/shard_map/psum | solution.py:124
  322.7 1.7 broadcast_multiply_fusion.2
  324.4 1.9 broadcast_multiply_fusion.1
  326.2 1.9 broadcast_multiply_fusion
  328.1 0.0 all-to-all-done.1
  328.1 3.0 fusion.43
  (8 shorter events, 0.0 us)
Async XLA Ops:
  7.2 43.9 %copy-start = (bf16[1,1024,1024]{2,1,0:T(8,128)(2,1)S(1)}, bf16[1,1024,1024]{2,1,0:T(8,128)(2,1)}, u32[]{:S(2)}) copy-start(bf16[1,1024,1024]{2,1,0:T(8,128)(2,1)} %param.15) | copy-start | bytes 6291460
  14.4 18.1 %copy-start.5 = (bf16[1,1024,256]{2,1,0:T(8,128)(2,1)S(1)}, bf16[1,1024,256]{2,1,0:T(8,128)(2,1)}, u32[]{:S(2)}) copy-start(bf16[1,1024,256]{2,1,0:T(8,128)(2,1)} %param.18) | copy-start | bytes 1572868
  14.4 20.2 %copy-start.6 = (s32[1,128,8]{1,2,0:T(8,128)S(1)}, s32[1,128,8]{1,2,0:T(8,128)}, u32[]{:S(2)}) copy-start(s32[1,128,8]{1,2,0:T(8,128)} %param.16) | copy-start | bytes 12292
  14.4 20.4 %copy-start.7 = (s32[1,8,8]{2,1,0:T(8,128)S(1)}, s32[1,8,8]{2,1,0:T(8,128)}, u32[]{:S(2)}) copy-start(s32[1,8,8]{2,1,0:T(8,128)} %param.14) | copy-start | bytes 772
  15.5 35.6 %all-to-all-start = ((bf16[128,8,256]{2,1,0:T(8,128)(2,1)}), bf16[128,8,256]{2,1,0:T(8,128)(2,1)}, u32[]{:S(2)}, u32[]{:S(2)}) async-start(bf16[128,8,256]{2,1,0:T(8,128)(2,1)} %fusion.60), calls=%async_computation | async-start | bytes 1048576 | tf_op jit(solution)/shard_map/all_to_all | solution.py:101
  32.4 290.3 %all-reduce.4.cloned.1.call-start = ((), (), s32[]{:S(2)}) async-start(), calls=%async_computation.2 | async-start | bytes 2621440 | tf_op jit(solution)/shard_map/psum | solution.py:124
  33.5 22.4 %collective-permute-start = (bf16[1,1024,256]{1,2,0:T(8,128)(2,1)}, bf16[1,1024,256]{1,2,0:T(8,128)(2,1)S(1)}, u32[]{:S(2)}, u32[]{:S(2)}) collective-permute-start(bf16[1,1024,256]{1,2,0:T(8,128)(2,1)} %copy.21), channel_id=1, source_target_pairs={{0,128},{128,0},{1,129},{129,1},{2,130},{130,2},{3,131},{131,3},{4... | collective-permute-start | bytes 1572872 | tf_op jit(solution)/shard_map/ppermute | solution.py:12
  40.6 12.4 %copy-start.1 = (bf16[1,1024,256]{2,1,0:T(8,128)(2,1)S(1)}, bf16[1,1024,256]{2,1,0:T(8,128)(2,1)}, u32[]{:S(2)}) copy-start(bf16[1,1024,256]{2,1,0:T(8,128)(2,1)} %param.12) | copy-start | bytes 1572868
  51.1 1.9 copy-start.2
  51.1 2.4 copy-start.3
  53.5 0.9 copy-start.4
  53.5 0.9 copy-start.8
  53.5 1.2 copy-start.10
  53.5 1.2 copy-start.11
  54.7 1.1 copy-start.9
  69.4 258.7 %all-to-all-start.1 = ((bf16[128,8,256]{2,1,0:T(8,128)(2,1)}), bf16[128,8,256]{2,1,0:T(8,128)(2,1)S(1)}, u32[]{:S(2)}, u32[]{:S(2)}) async-start(bf16[128,8,256]{2,1,0:T(8,128)(2,1)} %bitcast.14), calls=%async_computation.1 | async-start | bytes 1048576 | tf_op jit(solution)/shard_map/all_to_all | solution.py:115
Sparse Core Ops, SparseCore 0:
  67.8 254.8 all-reduce.3
where the time goes:
time: 339 us; the launch traced here: 338 us
  waiting for transfers between devices  178 us (53%)
  blocking collectives  78.4 us (23%)
  starting transfers between devices  24.3 us (7%)
  matrix products  19.2 us (6%)
  between operations  14.3 us (4%)
  local copies, waits for them, and re-layouts  13.7 us (4%)
  other arithmetic  10.2 us (3%)
    psum x1, waiting for transfers between devices, local(): lax.psum((grads[0], grads[1], grads[2], grads[3], grads[4]), ('view', 'do...  167 us
    psum x1, blocking collectives, local(): lax.psum((grads[0], grads[1], grads[2], grads[3], grads[4]), ('view', 'do...  78.4 us
    all_to_all x1, starting transfers between devices, local(): lax.all_to_all(outgoing, 'dom', split_axis=0, concat_axis=0, tiled=True)  16.9 us
    all_to_all x1, waiting for transfers between devices, local(): lax.all_to_all(outgoing, 'dom', split_axis=0, concat_axis=0, tiled=True)  10.5 us
  transfers between devices with their start and end apart: 4, of which 2 were waited for; matrix products, arithmetic and copies ran while one was open for 6% of the time, Pallas kernels for 0%

commit v1 on v0

v1 whole, which is shorter than its diff:
```python
import jax
import jax.numpy as jnp
from jax import lax
from jax.experimental import pallas as pl
from jax.experimental.pallas import tpu as pltpu
from jax.sharding import PartitionSpec as P

f32, bf16, i32 = jnp.float32, jnp.bfloat16, jnp.int32
NY, NX, NZ = 4, 4, 8
NODES, WIDE, PEERS, SLOTS = 1024, 256, 128, 8
ORDER = (2, 1, 3, 0)
MESH = pl.DeviceIdType.MESH
MAIN = 80
loss_scale = 64.0


def dot(a, b, ca=1, cb=0):
    return lax.dot_general(a, b, (((ca,), (cb,)), ((), ())), preferred_element_type=f32)


def iota(shape, dim):
    return lax.broadcasted_iota(i32, shape, dim)


def gelu_both(v):
    k = 0.7978845608028654
    c = 0.044715
    v2 = v * v
    h = 0.5 + 0.5 * jnp.tanh(v * (k + (k * c) * v2))
    value = v * h
    slope = h + value * (1.0 - h) * (2.0 * k + (6.0 * k * c) * v2)
    return value, slope


def pack(g):
    rows = g.shape[0] // 8
    left = g[:, :128].reshape(rows, 8, 128)
    right = g[:, 128:].reshape(rows, 8, 128)
    return jnp.concatenate([left, right], axis=1).astype(bf16)


def unpack(c):
    rows = c.shape[0]
    wide = c.astype(f32)
    left = wide[:, :8].reshape(rows * 8, 128)
    right = wide[:, 8:].reshape(rows * 8, 128)
    return jnp.concatenate([left, right], axis=1).astype(bf16)


def block(i, size=256):
    return pl.ds(pl.multiple_of(i * size, size), size)


def kernel(
    feat_hbm, adj_hbm, keep_ref, halo_hbm, rows_ref, count_ref, target_hbm,
    we_ref, be_ref, wi_ref, bi_ref, wo_ref,
    fg_ref, ew_ref, eb_ref, iw_ref, ib_ref, ow_ref,
    feat, adj, halo, other, adj_t, halo_t, sel,
    acc, aggr, emb, hid, pgrad, hgrad, egrad, agrad, back,
    o1, a1, b1, c1, o2, a2, b2, c2,
    gf, m1, n1, m2, n2, m3, n3, m4, n4, pf,
    lsem, tsem,
    zs1, zr1, xs1, xr1, ys1, yr1, zs2, zr2, xs2, xr2, ys2, yr2,
    rvs, rxs, rxr, rys, ryr, rzs, rzr, gys, gyr, gxs, gxr,
):
    v = lax.axis_index("view")
    d = lax.axis_index("dom")
    z = d % NZ
    x = (d // NZ) % NX
    y = d // (NZ * NX)

    def at_z(c):
        return (v, (y * NX + x) * NZ + (z + c) % NZ)

    def at_x(c):
        return (v, (y * NX + (x + c) % NX) * NZ + z)

    def at_y(c):
        return (v, (((y + c) % NY) * NX + x) * NZ + z)

    mate = (1 - v, d)

    barrier = pltpu.get_barrier_semaphore()
    pl.semaphore_signal(barrier, inc=1, device_id=mate, device_id_type=MESH)
    for c in range(1, NY):
        pl.semaphore_signal(barrier, inc=1, device_id=at_y(c), device_id_type=MESH)
    for c in range(1, NX):
        pl.semaphore_signal(barrier, inc=1, device_id=at_x(c), device_id_type=MESH)
    for c in range(1, NZ):
        pl.semaphore_signal(barrier, inc=1, device_id=at_z(c), device_id_type=MESH)

    loads = [
        pltpu.make_async_copy(src, dst, lsem.at[i])
        for i, (src, dst) in enumerate(((feat_hbm, feat), (adj_hbm, adj), (halo_hbm, halo)))
    ]
    for item in loads:
        item.start()

    def remote(src, dst, ssem, rsem, device):
        return pltpu.make_async_remote_copy(
            src_ref=src, dst_ref=dst, send_sem=ssem, recv_sem=rsem,
            device_id=device, device_id_type=MESH,
        )

    class Exchange:
        def __init__(self, o, a, b, c, zs, zr, xs, xr, ys, yr):
            self.o, self.a, self.b, self.c = o, a, b, c
            self.zs, self.zr, self.xs, self.xr, self.ys, self.yr = zs, zr, xs, xr, ys, yr

        def z_copy(self, cy, c, slot):
            return remote(
                self.o.at[cy, :, (z + c) % NZ], self.a.at[cy, slot],
                self.zs.at[cy, c], self.zr.at[cy, c], at_z(c),
            )

        def x_home(self, cy, slot):
            return self.c.at[y, slot] if cy == 0 else self.b.at[cy - 1, slot]

        def x_copy(self, cy, c, slot):
            return remote(
                self.a.at[cy, :, (x + c) % NX], self.x_home(cy, slot),
                self.xs.at[cy, c], self.xr.at[cy, c], at_x(c),
            )

        def y_copy(self, cy, slot):
            return remote(
                self.b.at[cy - 1], self.c.at[slot],
                self.ys.at[cy], self.yr.at[cy], at_y(cy),
            )

        def send_z(self, cy):
            @pl.loop(1, NZ)
            def _(c):
                self.z_copy(cy, c, z).start()

            self.a[cy, z] = self.o[cy, :, z]

        def z_to_x(self, cy):
            @pl.loop(1, NZ)
            def _(c):
                self.z_copy(cy, c, (z - c + NZ) % NZ).wait_recv()

            for c in range(1, NX):
                self.x_copy(cy, c, x).start()
            self.x_home(cy, x)[...] = self.a[cy, :, x]

        def x_to_y(self, cy):
            for c in range(1, NX):
                self.x_copy(cy, c, (x - c + NX) % NX).wait_recv()
            if cy:
                self.y_copy(cy, y).start()

        def arrived(self, cy):
            source = (y - cy + NY) % NY
            if cy:
                self.y_copy(cy, source).wait_recv()
            return source, unpack(self.c[source].reshape(NX * NZ, 16, 128))

        def finish(self):
            for cy in ORDER:
                @pl.loop(1, NZ)
                def _(c):
                    self.z_copy(cy, c, z).wait_send()

                for c in range(1, NX):
                    self.x_copy(cy, c, x).wait_send()
                if cy:
                    self.y_copy(cy, y).wait_send()

    first = Exchange(o1, a1, b1, c1, zs1, zr1, xs1, xr1, ys1, yr1)
    second = Exchange(o2, a2, b2, c2, zs2, zr2, xs2, xr2, ys2, yr2)

    masked = jnp.where(iota((SLOTS, PEERS), 0) < count_ref[...], rows_ref[...], -1)
    code = jnp.concatenate([(masked >> 5).astype(f32), (masked & 31).astype(f32)], axis=0).astype(bf16)

    def outgoing(cy):
        there = (y + cy) % NY
        place = iota((256, PEERS), 0) // 8 + there * (NX * NZ)
        spread = jnp.where(iota((256, PEERS), 1) == place, 1.0, 0.0).astype(bf16)
        parts = dot(spread, code, 1, 1)
        lane = iota((256, 16), 1)
        weight = jnp.where(
            (lane & 7) == (iota((256, 16), 0) & 7), jnp.where(lane < 8, 32.0, 1.0), 0.0
        )
        row = jnp.sum(parts * weight, axis=1, keepdims=True).astype(i32)
        hot = jnp.where(iota((256, NODES), 1) == row, 1.0, 0.0).astype(bf16)
        o1[cy] = pack(dot(hot, feat[...])).reshape(NX, NZ, 16, 128)

    loads[0].wait()
    outgoing(ORDER[0])
    pl.semaphore_wait(barrier, NZ + NX + NY - 2)
    first.send_z(ORDER[0])
    for cy in ORDER[1:]:
        outgoing(cy)
        first.send_z(cy)
    swap = remote(target_hbm, other, tsem.at[0], tsem.at[1], mate)
    swap.start()

    loads[1].wait()

    @pl.loop(0, 8)
    def _(i):
        for j in range(8):
            keep = keep_ref[i, j].astype(f32)
            tile = adj[block(i, 128), j * 128 : (j + 1) * 128].astype(f32)
            adj[block(i, 128), j * 128 : (j + 1) * 128] = (tile * keep).astype(bf16)

    @pl.loop(0, 4)
    def _(r):
        acc[block(r), :] = dot(adj[block(r), :], feat[...])

    first.z_to_x(2)
    loads[2].wait()

    def transpose(source, target):
        @pl.loop(0, 4)
        def _(r):
            for q in range(4):
                target[q * 256 : (q + 1) * 256, block(r)] = source[
                    block(r), q * 256 : (q + 1) * 256
                ].T

    transpose(halo, halo_t)
    first.z_to_x(1)
    first.x_to_y(2)
    transpose(adj, adj_t)
    first.z_to_x(3)
    first.x_to_y(1)

    spread = jnp.where(iota((PEERS, NODES), 1) // 8 == iota((PEERS, NODES), 0), 1.0, 0.0).astype(bf16)
    parts = dot(code, spread)
    slot = iota((16, NODES), 0)
    weight = jnp.where((slot & 7) == (iota((16, NODES), 1) & 7), jnp.where(slot < 8, 32.0, 1.0), 0.0)
    row = jnp.sum(parts * weight, axis=0, keepdims=True).astype(i32)

    @pl.loop(0, 4)
    def _(r):
        sel[block(r), :] = jnp.where(iota((256, NODES), 0) + r * 256 == row, 1.0, 0.0).astype(bf16)

    first.z_to_x(0)
    first.x_to_y(3)

    def gather_in(cy):
        source, rows = first.arrived(cy)

        @pl.loop(0, 4)
        def _(r):
            acc[block(r), :] += dot(halo[block(r), block(source)], rows)

    gather_in(2)
    gather_in(1)
    first.x_to_y(0)
    gather_in(0)
    gather_in(3)
    swap.wait_recv()

    @pl.loop(0, 4)
    def _(r):
        at = block(r)
        agg = acc[at, :].astype(bf16)
        aggr[at, :] = agg
        value, enc_slope = gelu_both(dot(agg, we_ref[...]) + be_ref[...])
        embed = value.astype(bf16)
        emb[at, :] = embed
        value, in_slope = gelu_both(dot(embed, wi_ref[...]) + bi_ref[...])
        hidden = value.astype(bf16)
        hid[at, :] = hidden
        pred = dot(hidden, wo_ref[...])
        goal = other[at, :].astype(f32)
        squares_p = jnp.sum(pred * pred, axis=1, keepdims=True) + 1e-06
        squares_t = jnp.sum(goal * goal, axis=1, keepdims=True) + 1e-06
        over = 1.0 / jnp.sqrt(squares_p * squares_t)
        cosine = jnp.sum(pred * goal, axis=1, keepdims=True) * over
        pg = (
            (-2.0 * loss_scale * over) * goal + (2.0 * loss_scale * cosine / squares_p) * pred
        ).astype(bf16)
        pgrad[at, :] = pg
        hg = (in_slope * dot(pg, wo_ref[...], 1, 1)).astype(bf16)
        hgrad[at, :] = hg
        eg = (enc_slope * dot(hg, wi_ref[...], 1, 1)).astype(bf16)
        egrad[at, :] = eg
        agrad[at, :] = dot(eg, we_ref[...], 1, 1).astype(bf16)

    for cy in ORDER:
        there = (y + cy) % NY
        o2[cy] = pack(dot(halo_t[block(there), :], agrad[...])).reshape(NX, NZ, 16, 128)
        second.send_z(cy)

    pairs = (
        (hid, 0, pgrad, 0), (hid, 1, pgrad, 0), (emb, 0, hgrad, 0), (emb, 0, hgrad, 1), (aggr, 0, egrad, 0),
    )
    for i, (left, lq, right, rq) in enumerate(pairs):
        grad = dot(
            left[:, lq * 256 : (lq + 1) * 256], right[:, rq * 256 : (rq + 1) * 256], 0, 0
        )
        gf[i * 512 : i * 512 + 256, :] = grad[:, :128]
        gf[i * 512 + 256 : (i + 1) * 512, :] = grad[:, 128:]
    enc_bias = jnp.sum(egrad[...].astype(f32), axis=0, keepdims=True)
    in_bias = jnp.sum(hgrad[...].astype(f32), axis=0, keepdims=True)
    bias = jnp.concatenate(
        [enc_bias[:, :128], enc_bias[:, 128:]]
        + [in_bias[:, q * 128 : (q + 1) * 128] for q in range(4)]
        + [jnp.zeros((10, 128), f32)],
        axis=0,
    )
    half = 16 * MAIN
    m1[:half, :] = gf[block(1 - v, half), :].astype(bf16)
    m1[half:, :] = bias.astype(bf16)
    across = remote(m1, n1, rvs.at[0], rvs.at[1], mate)
    across.start()

    second.z_to_x(2)

    @pl.loop(0, 4)
    def _(r):
        back[block(r), :] = dot(adj_t[block(r), :], agrad[...])

    across.wait_recv()
    bias = m1[half:, :].astype(f32) + n1[half:, :].astype(f32)

    part = 4 * MAIN
    own = gf[block(v, half), :] + n1[:half, :].astype(f32)
    for q in range(NX):
        m2[q, :part, :] = own[q * part : (q + 1) * part, :].astype(bf16)
        m2[q, part:, :] = bias.astype(bf16)

    def over_x(c, slot):
        return remote(m2.at[(x + c) % NX], n2.at[slot], rxs.at[c], rxr.at[c], at_x(c))

    for c in range(1, NX):
        over_x(c, x).start()
    n2[x] = m2[x]

    second.z_to_x(1)
    second.x_to_y(2)
    second.z_to_x(3)
    second.x_to_y(1)

    for c in range(1, NX):
        over_x(c, (x - c + NX) % NX).wait_recv()
    total = sum(n2[q].astype(f32) for q in range(NX))
    for q in range(NY):
        m3[q, :MAIN, :] = total[q * MAIN : (q + 1) * MAIN, :].astype(bf16)
        m3[q, MAIN:, :] = total[part:, :].astype(bf16)

    def over_y(c, slot):
        return remote(m3.at[(y + c) % NY], n3.at[slot], rys.at[c], ryr.at[c], at_y(c))

    for c in range(1, NY):
        over_y(c, y).start()
    n3[y] = m3[y]

    second.z_to_x(0)
    second.x_to_y(3)

    for c in range(1, NY):
        over_y(c, (y - c + NY) % NY).wait_recv()
    m4[...] = sum(n3[q].astype(f32) for q in range(NY)).astype(bf16)

    def over_z(c, slot):
        return remote(m4, n4.at[slot], rzs.at[c], rzr.at[c], at_z(c))

    @pl.loop(1, NZ)
    def _(c):
        over_z(c, z).start()

    n4[z] = m4[...]

    def scatter_in(cy):
        source, rows = second.arrived(cy)

        @pl.loop(0, 4)
        def _(r):
            back[block(r), :] += dot(sel[block(r), block(source)], rows)

    scatter_in(2)

    @pl.loop(1, NZ)
    def _(c):
        over_z(c, (z - c + NZ) % NZ).wait_recv()

    scale = 1.0 / (2.0 * NODES * PEERS) ** 0.5
    total = sum(n4[q].astype(f32) for q in range(NZ)) * scale
    pf[v, x, y] = total[:MAIN, :].astype(bf16)

    def share_y(c, slot):
        return remote(pf.at[v, x, y], pf.at[v, x, slot], gys.at[c], gyr.at[c], at_y(c))

    for c in range(1, NY):
        share_y(c, y).start()
    eb_ref[...] = jnp.concatenate([total[MAIN + q : MAIN + q + 1, :] for q in range(2)], axis=1)
    ib_ref[...] = jnp.concatenate([total[MAIN + 2 + q : MAIN + 3 + q, :] for q in range(4)], axis=1)

    scatter_in(1)
    second.x_to_y(0)
    scatter_in(0)

    for c in range(1, NY):
        share_y(c, (y - c + NY) % NY).wait_recv()

    def share_x(c, slot):
        return remote(pf.at[v, x], pf.at[v, slot], gxs.at[c], gxr.at[c], at_x(c))

    for c in range(1, NX):
        share_x(c, x).start()

    scatter_in(3)
    fg_ref[...] = back[...].astype(bf16)

    for c in range(1, NX):
        share_x(c, (x - c + NX) % NX).wait_recv()
    share = remote(pf.at[v], pf.at[v], rvs.at[2], rvs.at[3], mate)
    share.start()
    remote(pf.at[v], pf.at[1 - v], rvs.at[2], rvs.at[3], mate).wait_recv()

    flat = pf[...].reshape(2 * half, 128)
    for i in range(2):
        for q in range(2):
            at = i * 512 + q * 256
            ow_ref[i * 256 : (i + 1) * 256, q * 128 : (q + 1) * 128] = flat[at : at + 256].astype(f32)
            at += 1024
            col = i * 256 + q * 128
            iw_ref[:, col : col + 128] = flat[at : at + 256].astype(f32)
    for q in range(2):
        at = 2048 + q * 256
        ew_ref[:, q * 128 : (q + 1) * 128] = flat[at : at + 256].astype(f32)

    swap.wait_send()
    first.finish()
    second.finish()
    across.wait_send()
    for c in range(1, NX):
        over_x(c, x).wait_send()
        over_y(c, y).wait_send()
        share_y(c, y).wait_send()
        share_x(c, x).wait_send()

    @pl.loop(1, NZ)
    def _(c):
        over_z(c, z).wait_send()

    share.wait_send()


def local(
    features, local_adjacency, tile_keep, halo_adjacency, send_rows, send_count, target,
    w_encoder, b_encoder, w_predict_in, b_predict_in, w_predict_out,
):
    vmem = pl.BlockSpec(memory_space=pltpu.VMEM)
    anywhere = pl.BlockSpec(memory_space=pl.ANY)
    rows = jnp.swapaxes(send_rows[0], 0, 1)
    dma = pltpu.SemaphoreType.DMA
    v16 = lambda *shape: pltpu.VMEM(shape, bf16)
    v32 = lambda *shape: pltpu.VMEM(shape, f32)
    exchange = [
        v16(NY, NX, NZ, 16, 128), v16(NY, NZ, NX, 16, 128),
        v16(NY - 1, NX, NZ, 16, 128), v16(NY, NX, NZ, 16, 128),
    ]
    exchange_sems = [dma((NY, NZ)), dma((NY, NZ)), dma((NY, NX)), dma((NY, NX)), dma((NY,)), dma((NY,))]
    outs = pl.pallas_call(
        kernel,
        out_shape=(
            jax.ShapeDtypeStruct((NODES, WIDE), bf16),
            jax.ShapeDtypeStruct((WIDE, WIDE), f32),
            jax.ShapeDtypeStruct((1, WIDE), f32),
            jax.ShapeDtypeStruct((WIDE, 2 * WIDE), f32),
            jax.ShapeDtypeStruct((1, 2 * WIDE), f32),
            jax.ShapeDtypeStruct((2 * WIDE, WIDE), f32),
        ),
        in_specs=[
            anywhere, anywhere, pl.BlockSpec(memory_space=pltpu.SMEM), anywhere, vmem, vmem, anywhere,
            vmem, vmem, vmem, vmem, vmem,
        ],
        out_specs=(vmem,) * 6,
        scratch_shapes=[
            v16(NODES, WIDE), v16(NODES, NODES), v16(NODES, NODES), v16(NODES, WIDE),
            v16(NODES, NODES), v16(NODES, NODES), v16(NODES, NODES),
            v32(NODES, WIDE), v16(NODES, WIDE), v16(NODES, WIDE), v16(NODES, 2 * WIDE),
            v16(NODES, WIDE), v16(NODES, 2 * WIDE), v16(NODES, WIDE), v16(NODES, WIDE), v32(NODES, WIDE),
        ]
        + exchange + exchange
        + [
            v32(32 * MAIN, 128), v16(16 * MAIN + 16, 128), v16(16 * MAIN + 16, 128),
            v16(NX, 4 * MAIN + 16, 128), v16(NX, 4 * MAIN + 16, 128),
            v16(NY, MAIN + 16, 128), v16(NY, MAIN + 16, 128),
            v16(MAIN + 16, 128), v16(NZ, MAIN + 16, 128), v16(2, NX, NY, MAIN, 128),
            dma((3,)), dma((2,)),
        ]
        + exchange_sems + exchange_sems
        + [dma((4,)), dma((NX,)), dma((NX,)), dma((NY,)), dma((NY,)), dma((NZ,)), dma((NZ,)),
           dma((NY,)), dma((NY,)), dma((NX,)), dma((NX,))],
        compiler_params=pltpu.CompilerParams(
            collective_id=0, has_side_effects=True, vmem_limit_bytes=56 * 1024 * 1024
        ),
    )(
        features[0], local_adjacency[0], tile_keep[0], halo_adjacency[0], rows, send_count, target[0],
        w_encoder, b_encoder[None], w_predict_in, b_predict_in[None], w_predict_out,
    )
    feature_grad, enc, enc_bias, into, in_bias, out = outs
    return feature_grad[None], enc, enc_bias[0], into, in_bias[0], out


def solution(mesh):
    split = P("view", "dom", None)
    return jax.shard_map(
        local,
        mesh=mesh,
        in_specs=(split, split, split, split, split, P("view", "dom"), split, P(), P(), P(), P(), P()),
        out_specs=(split, P(), P(), P(), P(), P()),
        check_vma=False,
    )
```

time: 339 us -> 87.6 us (0.26)
  waiting for transfers between devices: 178 us -> 0 us
  Pallas kernels: 0 us -> 78.7 us
  blocking collectives: 78.4 us -> 0 us
  starting transfers between devices: 24.3 us -> 0 us
  matrix products: 19.2 us -> 0 us
  between operations: 14.3 us -> 0.66 us
  other arithmetic: 10.2 us -> 0 us
  local copies, waits for them, and re-layouts: 13.7 us -> 8.07 us
    psum x1 -> x0, waiting for transfers between devices: 167 us -> none  [local(): lax.psum((grads[0], grads[1], grads[2], grads[3], grads[4]), ('view', 'do...]
    pallas_call x0 -> x1, Pallas kernels: none -> 78.7 us  [local(): pl.pallas_call(kernel, out_shape=(jax.ShapeDtypeStruct((NODES, WIDE), bf1...]
    psum x1 -> x0, blocking collectives: 78.4 us -> none  [local(): lax.psum((grads[0], grads[1], grads[2], grads[3], grads[4]), ('view', 'do...]
    all_to_all x2 -> x0, starting transfers between devices: 23.3 us -> none  [the longest x1 16.9 us: local(): lax.all_to_all(outgoing, 'dom', split_axis=0, concat_axis=0, tiled=True)]
    dot_general x14 -> x0, matrix products: 19.2 us -> none  [the longest x1 4.15 us: partition_pass(): jnp.dot(kept.T, aggregated_grad, preferred_element_type=jnp.float32)]
    all_to_all x2 -> x0, waiting for transfers between devices: 10.5 us -> none  [the longest x1 10.5 us: local(): lax.all_to_all(outgoing, 'dom', split_axis=0, concat_axis=0, tiled=True)]
    mul x5 -> x0, other arithmetic: 6.56 us -> none  [local(): item * factor]
    unnamed x26 -> x10, local copies, waits for them, and re-layouts: 1.78 us -> 8.07 us
  transfers between devices with their start and end apart: 4 -> 0, of which waited for: 2 -> 0; matrix products, arithmetic and copies ran while one was open for 6% -> 0% of each run, Pallas kernels for 0% -> 0%
where the time goes in v1:
time: 87.6 us; the launch traced here: 87.4 us
  Pallas kernels  78.7 us (90%)
  local copies, waits for them, and re-layouts  8.07 us (9%)
    pallas_call x1, Pallas kernels, local(): pl.pallas_call(kernel, out_shape=(jax.ShapeDtypeStruct((NODES, WIDE), bf1...  78.7 us
    unnamed x10, local copies, waits for them, and re-layouts  8.07 us

profile of v1, /device:TPU:1, one launch (start us, length us, event | category | flops | bytes accessed | tf_op | source)
XLA Modules:
  0.0 87.4 jit_solution(15423439465860061843)
XLA Ops:
  0.6 78.7 %shard_map.163 = (bf16[1024,256]{1,0:T(8,128)(2,1)}, f32[256,256]{1,0:T(8,128)}, f32[1,256]{1,0:T(1,128)}, f32[256,512]{1,0:T(8,128)}, f32[1,512]{1,0:T(1,128)}, /*index=5*/f32[512,256]{1,0:T(8,128)}) custom-call(bf16[1024,256]{1,0:T(8,128)(2,1)} %bitcast.15, bf16[1024,1024]{1,0:T(8,128)(2,1)} %bitcast.13, s32[8,8]{1,0:T(8,128)} %bitcast.18, ...), custom_call_target="tpu_custom_call" | custom-call | tf_op jit(solution)/shard_map/pallas_call | solution.py:460
  79.3 0.0 copy-start.1
  79.3 0.0 copy-start
  79.3 1.9 %copy.24 = bf16[1,1024,256]{2,1,0:T(8,128)(2,1)} copy(bf16[1,1024,256]{2,1,0:T(8,128)(2,1)} %bitcast.17) | data formatting | bytes 1048576
  81.3 1.7 %copy.25 = f32[256,256]{1,0:T(8,128)} copy(f32[256,256]{1,0:T(8,128)} %get-tuple-element.25) | data formatting | bytes 524288
  82.9 1.2 %copy.26 = f32[256]{0:T(256)} copy(f32[256]{0:T(256)} %bitcast.23) | data formatting | bytes 2048
  84.2 1.9 %copy.27 = f32[256,512]{1,0:T(8,128)} copy(f32[256,512]{1,0:T(8,128)} %get-tuple-element.27) | data formatting | bytes 1048576
  86.0 0.0 copy-done.1
  86.0 0.6 copy.28
  86.6 0.0 copy-done
  86.6 0.8 copy.29
Async XLA Ops:
  79.3 6.7 %copy-start.1 = (f32[1,512]{1,0:T(1,128)S(1)}, f32[1,512]{1,0:T(1,128)}, u32[]{:S(2)}) copy-start(f32[1,512]{1,0:T(1,128)} %get-tuple-element.16) | copy-start | bytes 6148
  79.3 7.3 %copy-start = (f32[512,256]{1,0:T(8,128)S(1)}, f32[512,256]{1,0:T(8,128)}, u32[]{:S(2)}) copy-start(f32[512,256]{1,0:T(8,128)} %get-tuple-element.29) | copy-start | bytes 1572868

commit v2 on v1

v2 whole, which is shorter than its diff:
```python
import jax
import jax.numpy as jnp
from jax import lax
from jax.experimental import pallas as pl
from jax.experimental.pallas import tpu as pltpu
from jax.sharding import PartitionSpec as P

f32, bf16, i32 = jnp.float32, jnp.bfloat16, jnp.int32
NY, NX, NZ = 4, 4, 8
NODES, WIDE, PEERS, SLOTS = 1024, 256, 128, 8
ORDER = (0, 2, 3, 1)
ROUTE = {0: "zx", 1: "zxy", 2: "yxz", 3: "yzx"}
MESH = pl.DeviceIdType.MESH
HALF = 1280
XF, YF, TINY = 48, 32, 16
loss_scale = 64.0


def dot(a, b, ca=1, cb=0):
    return lax.dot_general(a, b, (((ca,), (cb,)), ((), ())), preferred_element_type=f32)


def iota(shape, dim):
    return lax.broadcasted_iota(i32, shape, dim)


def gelu_both(v):
    k = 0.7978845608028654
    c = 0.044715
    v2 = v * v
    h = 0.5 + 0.5 * jnp.tanh(v * (k + (k * c) * v2))
    value = v * h
    slope = h + value * (1.0 - h) * (2.0 * k + (6.0 * k * c) * v2)
    return value, slope


def pack(g):
    rows = g.shape[0] // 8
    left = g[:, :128].reshape(rows, 8, 128)
    right = g[:, 128:].reshape(rows, 8, 128)
    return jnp.concatenate([left, right], axis=1).astype(bf16)


def unpack(c):
    rows = c.shape[0]
    wide = c.astype(f32)
    left = wide[:, :8].reshape(rows * 8, 128)
    right = wide[:, 8:].reshape(rows * 8, 128)
    return jnp.concatenate([left, right], axis=1).astype(bf16)


def block(i, size=256):
    return pl.ds(pl.multiple_of(i * size, size), size)


def kernel(
    feat_hbm, adj_hbm, keep_hbm, halo_hbm, rows_hbm, count_hbm, target_hbm,
    we_hbm, be_hbm, wi_hbm, bi_hbm, wo_hbm,
    fg_ref, pfa, pfb, tiny_ref,
    feat, adj, keep_ref, halo, rows_ref, count_ref, we_ref, be_ref, wi_ref, bi_ref, wo_ref,
    other, adj_t, halo_t, sel,
    acc, aggr, emb, hid, pgrad, hgrad, egrad, agrad, back,
    o1, p1, q1, c1, o2, p2, q2, c2,
    gf, m1, n1, ma, na, mb, nb, mc, nc, md, nd, me, ne, pz,
    lsem, tsem,
    zs1, zr1, xs1, xr1, ys1, yr1, zs2, zr2, xs2, xr2, ys2, yr2,
    vs, vr, gs, gr, hs, hr,
):
    v = lax.axis_index("view")
    d = lax.axis_index("dom")
    z = d % NZ
    x = (d // NZ) % NX
    y = d // (NZ * NX)

    def at_z(c):
        return (v, (y * NX + x) * NZ + (z + c) % NZ)

    def at_x(c):
        return (v, (y * NX + (x + c) % NX) * NZ + z)

    def at_y(c):
        return (v, (((y + c) % NY) * NX + x) * NZ + z)

    mate = (1 - v, d)

    barrier = pltpu.get_barrier_semaphore()
    pl.semaphore_signal(barrier, inc=1, device_id=mate, device_id_type=MESH)
    for c in range(1, NY):
        pl.semaphore_signal(barrier, inc=1, device_id=at_y(c), device_id_type=MESH)
    for c in range(1, NX):
        pl.semaphore_signal(barrier, inc=1, device_id=at_x(c), device_id_type=MESH)
    for c in range(1, NZ):
        pl.semaphore_signal(barrier, inc=1, device_id=at_z(c), device_id_type=MESH)

    loads = [
        pltpu.make_async_copy(src, dst, lsem.at[i])
        for i, (src, dst) in enumerate((
            (rows_hbm, rows_ref), (count_hbm, count_ref), (feat_hbm, feat),
            (keep_hbm, keep_ref), (adj_hbm, adj), (halo_hbm, halo),
            (we_hbm, we_ref), (be_hbm, be_ref), (wi_hbm, wi_ref), (bi_hbm, bi_ref), (wo_hbm, wo_ref),
        ))
    ]
    for item in loads:
        item.start()

    def remote(src, dst, ssem, rsem, device):
        return pltpu.make_async_remote_copy(
            src_ref=src, dst_ref=dst, send_sem=ssem, recv_sem=rsem,
            device_id=device, device_id_type=MESH,
        )

    class Exchange:
        def __init__(self, o, p, q, c, zs, zr, xs, xr, ys, yr):
            self.o, self.p, self.q, self.c = o, p, q, c
            self.zs, self.zr, self.xs, self.xr, self.ys, self.yr = zs, zr, xs, xr, ys, yr

        def held(self, cy, k, last):
            if k == len(ROUTE[cy]):
                return self.c.at[last]
            return (self.o.at[cy], self.p.at[cy], self.q.at[cy - 1] if cy else None)[k]

        def copy(self, cy, k, c, back):
            line = ROUTE[cy][k]
            source = (y - cy + NY) % NY
            if line == "y":
                last = source if back else y
                return remote(
                    self.held(cy, k, None), self.held(cy, k + 1, last), self.ys.at[cy], self.yr.at[cy], at_y(cy)
                )
            here, there = self.held(cy, k, None), self.held(cy, k + 1, source)
            if line == "z":
                slot = (z - c + NZ) % NZ if back else z
                return remote(
                    here.at[:, (z + c) % NZ], there.at[:, slot], self.zs.at[cy, c], self.zr.at[cy, c], at_z(c)
                )
            slot = (x - c + NX) % NX if back else x
            return remote(here.at[(x + c) % NX], there.at[slot], self.xs.at[cy, c], self.xr.at[cy, c], at_x(c))

        def each(self, cy, k, act):
            line = ROUTE[cy][k]
            if line == "y":
                act(cy)
            elif line == "x":
                for c in range(1, NX):
                    act(c)
            else:
                pl.loop(1, NZ)(act)

        def start(self, cy, k):
            self.each(cy, k, lambda c: self.copy(cy, k, c, False).start())
            line = ROUTE[cy][k]
            if line != "y":
                here, there = self.held(cy, k, None), self.held(cy, k + 1, (y - cy + NY) % NY)
                if line == "z":
                    there[:, z] = here[:, z]
                else:
                    there[x] = here[x]

        def wait(self, cy, k):
            self.each(cy, k, lambda c: self.copy(cy, k, c, True).wait_recv())

        def step(self, cy, k):
            self.wait(cy, k - 1)
            self.start(cy, k)

        def arrived(self, cy):
            self.wait(cy, len(ROUTE[cy]) - 1)
            source = (y - cy + NY) % NY
            return source, unpack(self.c[source].reshape(NX * NZ, 16, 128))

        def finish(self):
            for cy in ORDER:
                for k in range(len(ROUTE[cy])):
                    self.each(cy, k, lambda c: self.copy(cy, k, c, False).wait_send())

    first = Exchange(o1, p1, q1, c1, zs1, zr1, xs1, xr1, ys1, yr1)
    second = Exchange(o2, p2, q2, c2, zs2, zr2, xs2, xr2, ys2, yr2)

    loads[0].wait()
    loads[1].wait()

    masked = jnp.where(iota((SLOTS, PEERS), 0) < count_ref[...], rows_ref[...], -1)
    code = jnp.concatenate([(masked >> 5).astype(f32), (masked & 31).astype(f32)], axis=0).astype(bf16)

    def outgoing(cy):
        there = (y + cy) % NY
        place = iota((256, PEERS), 0) // 8 + there * (NX * NZ)
        spread = jnp.where(iota((256, PEERS), 1) == place, 1.0, 0.0).astype(bf16)
        parts = dot(spread, code, 1, 1)
        lane = iota((256, 16), 1)
        weight = jnp.where(
            (lane & 7) == (iota((256, 16), 0) & 7), jnp.where(lane < 8, 32.0, 1.0), 0.0
        )
        row = jnp.sum(parts * weight, axis=1, keepdims=True).astype(i32)
        hot = jnp.where(iota((256, NODES), 1) == row, 1.0, 0.0).astype(bf16)
        o1[cy] = pack(dot(hot, feat[...])).reshape(NX, NZ, 16, 128)

    loads[2].wait()
    outgoing(ORDER[0])
    pl.semaphore_wait(barrier, NZ + NX + NY - 2)
    first.start(ORDER[0], 0)
    for cy in ORDER[1:]:
        outgoing(cy)
        first.start(cy, 0)
    swap = remote(target_hbm, other, tsem.at[0], tsem.at[1], mate)
    swap.start()

    for item in loads[3:5]:
        item.wait()

    @pl.loop(0, 8)
    def _(i):
        for j in range(8):
            keep = keep_ref[i, j].astype(f32)
            tile = adj[block(i, 128), j * 128 : (j + 1) * 128].astype(f32)
            adj[block(i, 128), j * 128 : (j + 1) * 128] = (tile * keep).astype(bf16)

    first.step(3, 1)

    @pl.loop(0, 4)
    def _(r):
        acc[block(r), :] = dot(adj[block(r), :], feat[...])

    first.step(0, 1)
    loads[5].wait()

    def transpose(source, target):
        @pl.loop(0, 4)
        def _(r):
            for q in range(4):
                target[q * 256 : (q + 1) * 256, block(r)] = source[
                    block(r), q * 256 : (q + 1) * 256
                ].T

    transpose(halo, halo_t)
    first.step(2, 1)
    transpose(adj, adj_t)
    first.step(1, 1)

    spread = jnp.where(iota((PEERS, NODES), 1) // 8 == iota((PEERS, NODES), 0), 1.0, 0.0).astype(bf16)
    parts = dot(code, spread)
    slot = iota((16, NODES), 0)
    weight = jnp.where((slot & 7) == (iota((16, NODES), 1) & 7), jnp.where(slot < 8, 32.0, 1.0), 0.0)
    row = jnp.sum(parts * weight, axis=0, keepdims=True).astype(i32)

    @pl.loop(0, 4)
    def _(r):
        sel[block(r), :] = jnp.where(iota((256, NODES), 0) + r * 256 == row, 1.0, 0.0).astype(bf16)

    def gather_in(cy):
        source, rows = first.arrived(cy)

        @pl.loop(0, 4)
        def _(r):
            acc[block(r), :] += dot(halo[block(r), block(source)], rows)

    first.step(2, 2)
    gather_in(0)
    first.step(1, 2)
    first.step(3, 2)
    for item in loads[6:]:
        item.wait()
    swap.wait_recv()
    gather_in(1)
    gather_in(3)
    gather_in(2)

    @pl.loop(0, 4)
    def _(r):
        at = block(r)
        agg = acc[at, :].astype(bf16)
        aggr[at, :] = agg
        value, enc_slope = gelu_both(dot(agg, we_ref[...]) + be_ref[...])
        embed = value.astype(bf16)
        emb[at, :] = embed
        value, in_slope = gelu_both(dot(embed, wi_ref[...]) + bi_ref[...])
        hidden = value.astype(bf16)
        hid[at, :] = hidden
        pred = dot(hidden, wo_ref[...])
        goal = other[at, :].astype(f32)
        squares_p = jnp.sum(pred * pred, axis=1, keepdims=True) + 1e-06
        squares_t = jnp.sum(goal * goal, axis=1, keepdims=True) + 1e-06
        over = 1.0 / jnp.sqrt(squares_p * squares_t)
        cosine = jnp.sum(pred * goal, axis=1, keepdims=True) * over
        pg = (
            (-2.0 * loss_scale * over) * goal + (2.0 * loss_scale * cosine / squares_p) * pred
        ).astype(bf16)
        pgrad[at, :] = pg
        hg = (in_slope * dot(pg, wo_ref[...], 1, 1)).astype(bf16)
        hgrad[at, :] = hg
        eg = (enc_slope * dot(hg, wi_ref[...], 1, 1)).astype(bf16)
        egrad[at, :] = eg
        agrad[at, :] = dot(eg, we_ref[...], 1, 1).astype(bf16)

    for cy in ORDER:
        there = (y + cy) % NY
        o2[cy] = pack(dot(halo_t[block(there), :], agrad[...])).reshape(NX, NZ, 16, 128)
        second.start(cy, 0)

    pairs = (
        (hid, 0, pgrad, 0), (hid, 1, pgrad, 0), (emb, 0, hgrad, 0), (emb, 0, hgrad, 1), (aggr, 0, egrad, 0),
    )
    for i, (left, lq, right, rq) in enumerate(pairs):
        grad = dot(
            left[:, lq * 256 : (lq + 1) * 256], right[:, rq * 256 : (rq + 1) * 256], 0, 0
        )
        gf[i * 512 : i * 512 + 256, :] = grad[:, :128]
        gf[i * 512 + 256 : (i + 1) * 512, :] = grad[:, 128:]
    enc_bias = jnp.sum(egrad[...].astype(f32), axis=0, keepdims=True)
    in_bias = jnp.sum(hgrad[...].astype(f32), axis=0, keepdims=True)
    bias = jnp.concatenate(
        [enc_bias[:, :128], enc_bias[:, 128:]]
        + [in_bias[:, q * 128 : (q + 1) * 128] for q in range(4)]
        + [jnp.zeros((10, 128), f32)],
        axis=0,
    )
    m1[:HALF, :] = gf[block(1 - v, HALF), :].astype(bf16)
    m1[HALF:, :] = bias.astype(bf16)
    across = remote(m1, n1, vs.at[0], vr.at[0], mate)
    across.start()

    second.step(3, 1)
    second.step(0, 1)

    across.wait_recv()
    bias = m1[HALF:, :].astype(f32) + n1[HALF:, :].astype(f32)
    own = gf[block(v, HALF), :] + n1[:HALF, :].astype(f32)

    for q in range(4):
        ma[q] = own[q * 4 * XF : (q + 1) * 4 * XF, :].astype(bf16)
        at = 16 * XF + q * 4 * YF
        mb[q, : 4 * YF, :] = own[at : at + 4 * YF, :].astype(bf16)
        mb[q, 4 * YF :, :] = bias.astype(bf16)

    def over_x(k, src, dst, c, back=False):
        slot = (x - c + NX) % NX if back else x
        return remote(src.at[(x + c) % NX], dst.at[slot], gs.at[k, c], gr.at[k, c], at_x(c))

    def over_y(k, src, dst, c, back=False):
        slot = (y - c + NY) % NY if back else y
        return remote(src.at[(y + c) % NY], dst.at[slot], gs.at[k, c], gr.at[k, c], at_y(c))

    for c in (2, 1, 3):
        over_x(0, ma, na, c).start()
        over_y(1, mb, nb, c).start()
    na[x] = ma[x]
    nb[y] = mb[y]

    @pl.loop(0, 4)
    def _(r):
        back[block(r), :] = dot(adj_t[block(r), :], agrad[...])

    second.step(2, 1)
    second.step(1, 1)

    for c in range(1, 4):
        over_x(0, ma, na, c, True).wait_recv()
        over_y(1, mb, nb, c, True).wait_recv()
    total = sum(na[q].astype(f32) for q in range(NX))
    for q in range(NY):
        mc[q] = total[q * XF : (q + 1) * XF, :].astype(bf16)
    total = sum(nb[q].astype(f32) for q in range(NY))
    for q in range(NX):
        md[q, :YF, :] = total[q * YF : (q + 1) * YF, :].astype(bf16)
        md[q, YF:, :] = total[4 * YF :, :].astype(bf16)
    for c in (2, 1, 3):
        over_y(2, mc, nc, c).start()
        over_x(3, md, nd, c).start()
    nc[y] = mc[y]
    nd[x] = md[x]

    second.step(2, 2)

    def scatter_in(cy):
        source, rows = second.arrived(cy)

        @pl.loop(0, 4)
        def _(r):
            back[block(r), :] += dot(sel[block(r), block(source)], rows)

    scatter_in(0)

    for c in range(1, 4):
        over_y(2, mc, nc, c, True).wait_recv()
        over_x(3, md, nd, c, True).wait_recv()
    total = sum(nc[q].astype(f32) for q in range(NY)).astype(bf16)
    for q in range(3):
        me[q] = total[q * 16 : (q + 1) * 16, :]
    total = sum(nd[q].astype(f32) for q in range(NX)).astype(bf16)
    for q in range(3):
        me[3 + q] = total[q * 16 : (q + 1) * 16, :]
    me[6:] = jnp.zeros((2, 16, 128), bf16)

    def to_z(c, back=False):
        slot = (z - c + NZ) % NZ if back else z
        return remote(me.at[(z + c) % NZ], ne.at[slot], hs.at[0, c], hr.at[0, c], at_z(c))

    @pl.loop(1, NZ)
    def _(c):
        to_z(c).start()

    ne[z] = me[z]
    second.step(1, 2)
    second.step(3, 2)

    @pl.loop(1, NZ)
    def _(c):
        to_z(c, True).wait_recv()

    scale = 1.0 / (2.0 * NODES * PEERS) ** 0.5
    pz[z] = (sum(ne[q].astype(f32) for q in range(NZ)) * scale).astype(bf16)

    def from_z(c, back=False):
        slot = (z - c + NZ) % NZ if back else z
        return remote(pz.at[z], pz.at[slot], hs.at[1, c], hr.at[1, c], at_z(c))

    @pl.loop(1, NZ)
    def _(c):
        from_z(c).start()

    scatter_in(1)

    @pl.loop(1, NZ)
    def _(c):
        from_z(c, True).wait_recv()

    for q in range(3):
        pfa[v, x, y, q * 16 : (q + 1) * 16, :] = pz[q]
    for q in range(2):
        pfb[v, y, x, q * 16 : (q + 1) * 16, :] = pz[3 + q]
    tiny_ref[...] = pz[5].astype(f32)

    def share_y(k, src, dst, c, back=False):
        slot = (y - c + NY) % NY if back else y
        return remote(src(y), dst(slot), gs.at[k, c], gr.at[k, c], at_y(c))

    def share_x(k, src, dst, c, back=False):
        slot = (x - c + NX) % NX if back else x
        return remote(src(x), dst(slot), gs.at[k, c], gr.at[k, c], at_x(c))

    xy = lambda q: pfa.at[v, x, q]
    yx = lambda q: pfb.at[v, y, q]
    for c in (2, 1, 3):
        share_y(4, xy, xy, c).start()
        share_x(5, yx, yx, c).start()
    scatter_in(3)
    for c in range(1, 4):
        share_y(4, xy, xy, c, True).wait_recv()
        share_x(5, yx, yx, c, True).wait_recv()
    xs = lambda q: pfa.at[v, q]
    ys = lambda q: pfb.at[v, q]
    for c in (2, 1, 3):
        share_x(6, xs, xs, c).start()
        share_y(7, ys, ys, c).start()

    def pass_a(c):
        q = (x - c + NX) % NX
        return remote(pfa.at[v, q], pfa.at[v, q], vs.at[1 + c], vr.at[1 + c], mate)

    def pass_b(c):
        q = (y - c + NY) % NY
        return remote(pfb.at[v, q], pfb.at[v, q], vs.at[5 + c], vr.at[5 + c], mate)

    def taken_a(c):
        q = (x - c + NX) % NX
        return remote(pfa.at[v, q], pfa.at[1 - v, q], vs.at[1 + c], vr.at[1 + c], mate)

    def taken_b(c):
        q = (y - c + NY) % NY
        return remote(pfb.at[v, q], pfb.at[1 - v, q], vs.at[5 + c], vr.at[5 + c], mate)

    pass_a(0).start()
    pass_b(0).start()
    scatter_in(2)
    fg_ref[...] = back[...].astype(bf16)
    for c in (1, 3, 2):
        share_x(6, xs, xs, c, True).wait_recv()
        pass_a(c).start()
        share_y(7, ys, ys, c, True).wait_recv()
        pass_b(c).start()
    for c in range(4):
        taken_a(c).wait_recv()
        taken_b(c).wait_recv()

    swap.wait_send()
    first.finish()
    second.finish()
    across.wait_send()
    for c in range(1, 4):
        over_x(0, ma, na, c).wait_send()
        over_y(1, mb, nb, c).wait_send()
        over_y(2, mc, nc, c).wait_send()
        over_x(3, md, nd, c).wait_send()
        share_y(4, xy, xy, c).wait_send()
        share_x(5, yx, yx, c).wait_send()
        share_x(6, xs, xs, c).wait_send()
        share_y(7, ys, ys, c).wait_send()
    for c in range(4):
        pass_a(c).wait_send()
        pass_b(c).wait_send()

    @pl.loop(1, NZ)
    def _(c):
        to_z(c).wait_send()
        from_z(c).wait_send()


def results(fg_in, pfa, pfb, tiny, fg_ref, ew_ref, eb_ref, iw_ref, ib_ref, ow_ref, sem):
    move = pltpu.make_async_copy(fg_in, fg_ref, sem)
    move.start()

    def rows(i):
        view, r = i // 5, i % 5
        src, at = (pfa, r * 256) if r < 3 else (pfb, (r - 3) * 256)
        return src[view, at : at + 256, :].astype(f32)

    for i in range(2):
        for q in range(2):
            ow_ref[i * 256 : (i + 1) * 256, q * 128 : (q + 1) * 128] = rows(2 * i + q)
            col = i * 256 + q * 128
            iw_ref[:, col : col + 128] = rows(4 + 2 * i + q)
    for q in range(2):
        ew_ref[:, q * 128 : (q + 1) * 128] = rows(8 + q)
        eb_ref[:, q * 128 : (q + 1) * 128] = tiny[q : q + 1, :]
    for q in range(4):
        ib_ref[:, q * 128 : (q + 1) * 128] = tiny[2 + q : 3 + q, :]
    move.wait()


def local(
    features, local_adjacency, tile_keep, halo_adjacency, send_rows, send_count, target,
    w_encoder, b_encoder, w_predict_in, b_predict_in, w_predict_out,
):
    vmem = pl.BlockSpec(memory_space=pltpu.VMEM)
    anywhere = pl.BlockSpec(memory_space=pl.ANY)
    dma = pltpu.SemaphoreType.DMA
    v16 = lambda *shape: pltpu.VMEM(shape, bf16)
    v32 = lambda *shape: pltpu.VMEM(shape, f32)
    exchange = [v16(NY, NX, NZ, 16, 128), v16(NY, NX, NZ, 16, 128), v16(NY - 1, NX, NZ, 16, 128), v16(NY, NX, NZ, 16, 128)]
    exchange_sems = [dma((NY, NZ)), dma((NY, NZ)), dma((NY, NX)), dma((NY, NX)), dma((NY,)), dma((NY,))]
    feature_grad, pfa, pfb, tiny = pl.pallas_call(
        kernel,
        out_shape=(
            jax.ShapeDtypeStruct((NODES, WIDE), bf16),
            jax.ShapeDtypeStruct((2, NX, NY, XF, 128), bf16),
            jax.ShapeDtypeStruct((2, NY, NX, YF, 128), bf16),
            jax.ShapeDtypeStruct((TINY, 128), f32),
        ),
        in_specs=[anywhere] * 12,
        out_specs=(vmem,) * 4,
        scratch_shapes=[
            v16(NODES, WIDE), v16(NODES, NODES), pltpu.SMEM((8, 8), i32), v16(NODES, NODES),
            pltpu.VMEM((SLOTS, PEERS), i32), pltpu.VMEM((1, PEERS), i32),
            v16(WIDE, WIDE), v32(1, WIDE), v16(WIDE, 2 * WIDE), v32(1, 2 * WIDE), v16(2 * WIDE, WIDE),
            v16(NODES, WIDE), v16(NODES, NODES), v16(NODES, NODES), v16(NODES, NODES),
            v32(NODES, WIDE), v16(NODES, WIDE), v16(NODES, WIDE), v16(NODES, 2 * WIDE),
            v16(NODES, WIDE), v16(NODES, 2 * WIDE), v16(NODES, WIDE), v16(NODES, WIDE), v32(NODES, WIDE),
        ]
        + exchange + exchange
        + [
            v32(2 * HALF, 128), v16(HALF + TINY, 128), v16(HALF + TINY, 128),
            v16(NX, 4 * XF, 128), v16(NX, 4 * XF, 128),
            v16(NY, 4 * YF + TINY, 128), v16(NY, 4 * YF + TINY, 128),
            v16(NY, XF, 128), v16(NY, XF, 128), v16(NX, YF + TINY, 128), v16(NX, YF + TINY, 128),
            v16(NZ, 16, 128), v16(NZ, 16, 128), v16(NZ, 16, 128),
            dma((11,)), dma((2,)),
        ]
        + exchange_sems + exchange_sems
        + [dma((9,)), dma((9,)), dma((8, 4)), dma((8, 4)), dma((2, NZ)), dma((2, NZ))],
        compiler_params=pltpu.CompilerParams(
            collective_id=0, has_side_effects=True, vmem_limit_bytes=48 * 1024 * 1024
        ),
    )(
        features[0], local_adjacency[0], tile_keep[0], halo_adjacency[0],
        jnp.swapaxes(send_rows[0], 0, 1), send_count, target[0],
        w_encoder, b_encoder[None], w_predict_in, b_predict_in[None], w_predict_out,
    )
    feature_grad, enc, enc_bias, into, in_bias, out = pl.pallas_call(
        results,
        out_shape=(
            jax.ShapeDtypeStruct((NODES, WIDE), bf16),
            jax.ShapeDtypeStruct((WIDE, WIDE), f32),
            jax.ShapeDtypeStruct((1, WIDE), f32),
            jax.ShapeDtypeStruct((WIDE, 2 * WIDE), f32),
            jax.ShapeDtypeStruct((1, 2 * WIDE), f32),
            jax.ShapeDtypeStruct((2 * WIDE, WIDE), f32),
        ),
        in_specs=[anywhere, vmem, vmem, vmem],
        out_specs=(anywhere,) + (vmem,) * 5,
        scratch_shapes=[pltpu.SemaphoreType.DMA(())],
    )(
        feature_grad, pfa.reshape(2, 16 * XF, 128), pfb.reshape(2, 16 * YF, 128), tiny
    )
    return feature_grad[None], enc, enc_bias[0], into, in_bias[0], out


def solution(mesh):
    split = P("view", "dom", None)
    return jax.shard_map(
        local,
        mesh=mesh,
        in_specs=(split, split, split, split, split, P("view", "dom"), split, P(), P(), P(), P(), P()),
        out_specs=(split, P(), P(), P(), P(), P()),
        check_vma=False,
    )
```

time: 87.6 us -> 109 us (1.24)
  Pallas kernels: 78.7 us -> 95.5 us
  local copies, waits for them, and re-layouts: 8.07 us -> 12.7 us
    pallas_call x0 -> x1, Pallas kernels: none -> 19.1 us  [local(): pl.pallas_call(results, out_shape=(jax.ShapeDtypeStruct((NODES, WIDE), bf...]
    unnamed x10 -> x30, local copies, waits for them, and re-layouts: 8.07 us -> 12.7 us
    pallas_call x1, Pallas kernels: 78.7 us -> 76.4 us  [local(): pl.pallas_call(kernel, out_shape=(jax.ShapeDtypeStruct((NODES, WIDE), bf1...]
where the time goes in v2:
time: 109 us
  Pallas kernels  95.5 us (88%)
  local copies, waits for them, and re-layouts  12.7 us (12%)
    pallas_call x1, Pallas kernels, local(): pl.pallas_call(kernel, out_shape=(jax.ShapeDtypeStruct((NODES, WIDE), bf1...  76.4 us
    pallas_call x1, Pallas kernels, local(): pl.pallas_call(results, out_shape=(jax.ShapeDtypeStruct((NODES, WIDE), bf...  19.1 us
    unnamed x30, local copies, waits for them, and re-layouts  12.7 us

profile of v2, /device:TPU:1, one launch (start us, length us, event | category | flops | bytes accessed | tf_op | source)
XLA Modules:
  0.0 108.9 jit_solution(4172231452701971083)
XLA Ops:
  0.6 0.0 copy-start
  0.6 1.6 %copy-done = bf16[1,1024,1024]{2,1,0:T(8,128)(2,1)S(1)} copy-done((bf16[1,1024,1024]{2,1,0:T(8,128)(2,1)S(1)}, bf16[1,1024,1024]{2,1,0:T(8,128)(2,1)}, u32[]{:S(2)}) %copy-start) | copy-done | bytes 2097176
  2.2 0.0 copy-start.1
  2.2 1.0 copy-done.1
  3.3 0.0 copy-start.2
  3.3 1.0 copy-done.2
  4.3 0.0 copy-start.5
  4.3 0.9 copy-done.5
  5.3 0.0 copy-start.6
  5.3 0.9 copy-done.6
  6.2 0.0 copy-start.8
  6.2 0.9 copy-done.8
  7.1 0.0 copy-start.10
  7.1 0.7 copy-done.10
  7.8 0.0 copy-start.11
  7.8 0.7 copy-done.11
  8.5 0.0 copy-start.12
  8.5 0.7 copy-done.12
  9.2 0.0 copy-start.13
  9.2 0.7 copy-done.13
  9.9 0.0 copy-start.14
  9.9 0.7 copy-done.14
  10.5 76.4 %shard_map.163 = (bf16[1024,256]{1,0:T(8,128)(2,1)S(1)}, bf16[2,4,4,48,128]{4,3,2,1,0:T(8,128)(2,1)S(1)}, bf16[2,4,4,32,128]{4,3,2,1,0:T(8,128)(2,1)S(1)}, f32[16,128]{1,0:T(8,128)S(1)}) custom-call(bf16[1024,256]{1,0:T(8,128)(2,1)S(1)} %bitcast.16, bf16[1024,1024]{1,0:T(8,128)(2,1)S(1)} %bitcast.15, s32[8,8]{1,0:T(8,128)S(1)} %bitcast.20, ...), custom_call_target="tpu_custom_call" | custom-call | tf_op jit(solution)/shard_map/pallas_call | solution.py:541
  86.9 0.0 copy-start.3
  86.9 0.8 copy-done.3
  87.7 0.0 copy-start.4
  87.7 0.7 copy-done.4
  88.4 0.0 copy-start.7
  88.4 0.7 copy-done.7
  89.2 0.0 copy-start.9
  89.2 0.6 copy-done.9
  89.7 19.1 %shard_map.164 = (bf16[1024,256]{1,0:T(8,128)(2,1)}, f32[256,256]{1,0:T(8,128)}, f32[1,256]{1,0:T(1,128)}, f32[256,512]{1,0:T(8,128)}, f32[1,512]{1,0:T(1,128)}, /*index=5*/f32[512,256]{1,0:T(8,128)}) custom-call(bf16[1024,256]{1,0:T(8,128)(2,1)} %copy-done.3, bf16[2,768,128]{2,1,0:T(8,128)(2,1)} %bitcast.18, bf16[2,512,128]{2,1,0:T(8,128)(2,1)} %bitcast.19, ...), custom_call_target="tpu_custom_call" | custom-call | tf_op jit(solution)/shard_map/pallas_call | solution.py:578
Async XLA Ops:
  0.6 1.6 %copy-start = (bf16[1,1024,1024]{2,1,0:T(8,128)(2,1)S(1)}, bf16[1,1024,1024]{2,1,0:T(8,128)(2,1)}, u32[]{:S(2)}) copy-start(bf16[1,1024,1024]{2,1,0:T(8,128)(2,1)} %param.13) | copy-start | bytes 6291460
  2.2 1.0 copy-start.1
  3.3 1.0 copy-start.2
  4.3 0.9 copy-start.5
  5.3 0.9 copy-start.6
  6.2 0.9 copy-start.8
  7.1 0.7 copy-start.10
  7.8 0.7 copy-start.11
  8.5 0.7 copy-start.12
  9.2 0.7 copy-start.13
  9.9 0.7 copy-start.14
  86.9 0.8 copy-start.3
  87.7 0.7 copy-start.4
  88.4 0.7 copy-start.7
  89.2 0.6 copy-start.9

commit v3 on v2

v3 whole, which is shorter than its diff:
```python
import jax
import jax.numpy as jnp
from jax import lax
from jax.experimental import pallas as pl
from jax.experimental.pallas import tpu as pltpu
from jax.sharding import PartitionSpec as P

f32, bf16, i32 = jnp.float32, jnp.bfloat16, jnp.int32
NY, NX, NZ = 4, 4, 8
NODES, WIDE, PEERS, SLOTS = 1024, 256, 128, 8
ORDER = (2, 1, 3, 0)
MESH = pl.DeviceIdType.MESH
PLANE = NX * NZ
HALF, PART, TINY = 1280, 80, 16
loss_scale = 64.0


def dot(a, b, ca=1, cb=0):
    return lax.dot_general(a, b, (((ca,), (cb,)), ((), ())), preferred_element_type=f32)


def iota(shape, dim):
    return lax.broadcasted_iota(i32, shape, dim)


def gelu_both(v):
    k = 0.7978845608028654
    c = 0.044715
    v2 = v * v
    h = 0.5 + 0.5 * jnp.tanh(v * (k + (k * c) * v2))
    value = v * h
    slope = h + value * (1.0 - h) * (2.0 * k + (6.0 * k * c) * v2)
    return value, slope


def pack(g):
    rows = g.shape[0] // 8
    left = g[:, :128].reshape(rows, 8, 128)
    right = g[:, 128:].reshape(rows, 8, 128)
    return jnp.concatenate([left, right], axis=1).astype(bf16)


def unpack(c):
    rows = c.shape[0]
    wide = c.astype(f32)
    left = wide[:, :8].reshape(rows * 8, 128)
    right = wide[:, 8:].reshape(rows * 8, 128)
    return jnp.concatenate([left, right], axis=1).astype(bf16)


def block(i, size=256):
    return pl.ds(pl.multiple_of(i * size, size), size)


def kernel(
    feat_hbm, adj_hbm, keep_hbm, halo_hbm, rows_hbm, count_hbm, target_hbm,
    we_hbm, be_hbm, wi_hbm, bi_hbm, wo_hbm,
    fg_ref, pf, tiny_ref,
    feat, adj, keep_ref, halo, rows_ref, count_ref, we_ref, be_ref, wi_ref, bi_ref, wo_ref,
    other, adj_t, halo_t, sel,
    acc, aggr, emb, hid, pgrad, hgrad, egrad, agrad, back,
    o1, c1, o2, c2,
    gf, m1, n1, ma, na, me, ne, pz,
    lsem, tsem, x_in, y_in,
    es1, er1, es2, er2, vs, vr, ps, pr, hs, hr,
):
    v = lax.axis_index("view")
    d = lax.axis_index("dom")
    z = d % NZ
    x = (d // NZ) % NX
    y = d // (NZ * NX)

    def at_z(c):
        return (v, (y * NX + x) * NZ + (z + c) % NZ)

    def at_x(c):
        return (v, (y * NX + (x + c) % NX) * NZ + z)

    def at_y(c):
        return (v, (((y + c) % NY) * NX + x) * NZ + z)

    def at_plane(c):
        return (v, (d + c * NZ) % PEERS)

    mate = (1 - v, d)

    barrier = pltpu.get_barrier_semaphore()
    pl.semaphore_signal(barrier, inc=1, device_id=mate, device_id_type=MESH)
    for c in range(1, NY):
        pl.semaphore_signal(barrier, inc=1, device_id=at_y(c), device_id_type=MESH)
    for c in range(1, NX):
        pl.semaphore_signal(barrier, inc=1, device_id=at_x(c), device_id_type=MESH)
    for c in range(1, NZ):
        pl.semaphore_signal(barrier, inc=1, device_id=at_z(c), device_id_type=MESH)

    loads = [
        pltpu.make_async_copy(src, dst, lsem.at[i])
        for i, (src, dst) in enumerate((
            (rows_hbm, rows_ref), (count_hbm, count_ref), (feat_hbm, feat),
            (keep_hbm, keep_ref), (adj_hbm, adj), (halo_hbm, halo),
            (we_hbm, we_ref), (be_hbm, be_ref), (wi_hbm, wi_ref), (bi_hbm, bi_ref), (wo_hbm, wo_ref),
        ))
    ]
    for item in loads:
        item.start()

    def remote(src, dst, ssem, rsem, device):
        return pltpu.make_async_remote_copy(
            src_ref=src, dst_ref=dst, send_sem=ssem, recv_sem=rsem,
            device_id=device, device_id_type=MESH,
        )

    class Exchange:
        def __init__(self, o, c, ss, rs):
            self.o, self.c, self.ss, self.rs = o, c, ss, rs

        def start(self, cy):
            there = (y + cy) % NY
            here = d % PLANE

            @pl.loop(0 if cy else 1, PLANE)
            def _(i):
                j = (here + i) % PLANE
                remote(
                    self.o.at[cy, j], self.c.at[y, here], self.ss.at[cy], self.rs.at[cy], (v, there * PLANE + j)
                ).start()

            if cy == 0:
                self.c[y, here] = self.o[0, here]

        def whole(self, cy):
            source = (y - cy + NY) % NY
            n = PLANE if cy else PLANE - 1
            return remote(
                self.o.at[cy, pl.ds(0, n)], self.c.at[source, pl.ds(0, n)], self.ss.at[cy], self.rs.at[cy], at_y(cy or 1)
            )

        def arrived(self, cy):
            self.whole(cy).wait_recv()
            source = (y - cy + NY) % NY
            return source, unpack(self.c[source])

        def finish(self):
            for cy in ORDER:
                self.whole(cy).wait_send()

    first = Exchange(o1, c1, es1, er1)
    second = Exchange(o2, c2, es2, er2)

    loads[0].wait()
    loads[1].wait()

    masked = jnp.where(iota((SLOTS, PEERS), 0) < count_ref[...], rows_ref[...], -1)
    code = jnp.concatenate([(masked >> 5).astype(f32), (masked & 31).astype(f32)], axis=0).astype(bf16)

    def outgoing(cy):
        there = (y + cy) % NY
        place = iota((256, PEERS), 0) // 8 + there * PLANE
        spread = jnp.where(iota((256, PEERS), 1) == place, 1.0, 0.0).astype(bf16)
        parts = dot(spread, code, 1, 1)
        lane = iota((256, 16), 1)
        weight = jnp.where(
            (lane & 7) == (iota((256, 16), 0) & 7), jnp.where(lane < 8, 32.0, 1.0), 0.0
        )
        row = jnp.sum(parts * weight, axis=1, keepdims=True).astype(i32)
        hot = jnp.where(iota((256, NODES), 1) == row, 1.0, 0.0).astype(bf16)
        o1[cy] = pack(dot(hot, feat[...]))

    loads[2].wait()
    outgoing(ORDER[0])
    pl.semaphore_wait(barrier, NZ + NX + NY - 2)
    for c in range(1, NX):
        pl.semaphore_signal(x_in, inc=1, device_id=at_x(c), device_id_type=MESH)
    outgoing(ORDER[1])
    pl.semaphore_wait(x_in, NX - 1)
    for c in range(1, NY):
        pl.semaphore_signal(y_in, inc=1, device_id=at_y(c), device_id_type=MESH)
    outgoing(ORDER[2])
    pl.semaphore_wait(y_in, NY - 1)
    for cy in ORDER[:3]:
        first.start(cy)
    outgoing(ORDER[3])
    first.start(ORDER[3])
    swap = remote(target_hbm, other, tsem.at[0], tsem.at[1], mate)
    swap.start()

    for item in loads[3:5]:
        item.wait()

    @pl.loop(0, 8)
    def _(i):
        for j in range(8):
            keep = keep_ref[i, j].astype(f32)
            tile = adj[block(i, 128), j * 128 : (j + 1) * 128].astype(f32)
            adj[block(i, 128), j * 128 : (j + 1) * 128] = (tile * keep).astype(bf16)

    @pl.loop(0, 4)
    def _(r):
        acc[block(r), :] = dot(adj[block(r), :], feat[...])

    loads[5].wait()

    def transpose(source, target):
        @pl.loop(0, 4)
        def _(r):
            for q in range(4):
                target[q * 256 : (q + 1) * 256, block(r)] = source[
                    block(r), q * 256 : (q + 1) * 256
                ].T

    transpose(halo, halo_t)
    transpose(adj, adj_t)

    spread = jnp.where(iota((PEERS, NODES), 1) // 8 == iota((PEERS, NODES), 0), 1.0, 0.0).astype(bf16)
    parts = dot(code, spread)
    slot = iota((16, NODES), 0)
    weight = jnp.where((slot & 7) == (iota((16, NODES), 1) & 7), jnp.where(slot < 8, 32.0, 1.0), 0.0)
    row = jnp.sum(parts * weight, axis=0, keepdims=True).astype(i32)

    @pl.loop(0, 4)
    def _(r):
        sel[block(r), :] = jnp.where(iota((256, NODES), 0) + r * 256 == row, 1.0, 0.0).astype(bf16)

    def gather_in(cy):
        source, rows = first.arrived(cy)

        @pl.loop(0, 4)
        def _(r):
            acc[block(r), :] += dot(halo[block(r), block(source)], rows)

    for item in loads[6:]:
        item.wait()
    swap.wait_recv()
    for cy in ORDER:
        gather_in(cy)

    @pl.loop(0, 4)
    def _(r):
        at = block(r)
        agg = acc[at, :].astype(bf16)
        aggr[at, :] = agg
        value, enc_slope = gelu_both(dot(agg, we_ref[...]) + be_ref[...])
        embed = value.astype(bf16)
        emb[at, :] = embed
        value, in_slope = gelu_both(dot(embed, wi_ref[...]) + bi_ref[...])
        hidden = value.astype(bf16)
        hid[at, :] = hidden
        pred = dot(hidden, wo_ref[...])
        goal = other[at, :].astype(f32)
        squares_p = jnp.sum(pred * pred, axis=1, keepdims=True) + 1e-06
        squares_t = jnp.sum(goal * goal, axis=1, keepdims=True) + 1e-06
        over = 1.0 / jnp.sqrt(squares_p * squares_t)
        cosine = jnp.sum(pred * goal, axis=1, keepdims=True) * over
        pg = (
            (-2.0 * loss_scale * over) * goal + (2.0 * loss_scale * cosine / squares_p) * pred
        ).astype(bf16)
        pgrad[at, :] = pg
        hg = (in_slope * dot(pg, wo_ref[...], 1, 1)).astype(bf16)
        hgrad[at, :] = hg
        eg = (enc_slope * dot(hg, wi_ref[...], 1, 1)).astype(bf16)
        egrad[at, :] = eg
        agrad[at, :] = dot(eg, we_ref[...], 1, 1).astype(bf16)

    pairs = (
        (hid, 0, pgrad, 0), (hid, 1, pgrad, 0), (emb, 0, hgrad, 0), (emb, 0, hgrad, 1), (aggr, 0, egrad, 0),
    )
    for i, (left, lq, right, rq) in enumerate(pairs):
        grad = dot(
            left[:, lq * 256 : (lq + 1) * 256], right[:, rq * 256 : (rq + 1) * 256], 0, 0
        )
        gf[i * 512 : i * 512 + 256, :] = grad[:, :128]
        gf[i * 512 + 256 : (i + 1) * 512, :] = grad[:, 128:]
    enc_bias = jnp.sum(egrad[...].astype(f32), axis=0, keepdims=True)
    in_bias = jnp.sum(hgrad[...].astype(f32), axis=0, keepdims=True)
    bias = jnp.concatenate(
        [enc_bias[:, :128], enc_bias[:, 128:]]
        + [in_bias[:, q * 128 : (q + 1) * 128] for q in range(4)]
        + [jnp.zeros((10, 128), f32)],
        axis=0,
    )
    m1[:HALF, :] = gf[block(1 - v, HALF), :].astype(bf16)
    m1[HALF:, :] = bias.astype(bf16)
    across = remote(m1, n1, vs.at[0], vr.at[0], mate)
    across.start()

    def return_rows(cy):
        there = (y + cy) % NY
        o2[cy] = pack(dot(halo_t[block(there), :], agrad[...]))
        second.start(cy)

    return_rows(ORDER[0])
    return_rows(ORDER[1])

    spot = d // NZ
    across.wait_recv()
    bias = (m1[HALF:, :].astype(f32) + n1[HALF:, :].astype(f32)).astype(bf16)

    @pl.loop(0, 16)
    def _(q):
        own = gf[pl.ds(v * HALF + q * PART, PART), :] + n1[pl.ds(q * PART, PART), :].astype(f32)
        ma[q, :PART, :] = own.astype(bf16)
        ma[q, PART:, :] = bias

    @pl.loop(1, 16)
    def _(c):
        remote(ma.at[(spot + c) % 16], na.at[spot], ps.at[0], pr.at[0], at_plane(c)).start()

    na[spot] = ma[spot]
    plane = remote(ma.at[pl.ds(0, 15)], na.at[pl.ds(0, 15)], ps.at[0], pr.at[0], at_plane(1))

    return_rows(ORDER[2])
    return_rows(ORDER[3])

    plane.wait_recv()
    total = sum(na[q].astype(f32) for q in range(16)).astype(bf16)
    for q in range(6):
        me[q] = total[q * 16 : (q + 1) * 16, :]
    me[6:] = jnp.zeros((2, 16, 128), bf16)

    @pl.loop(1, NZ)
    def _(c):
        remote(me.at[(z + c) % NZ], ne.at[z], hs.at[0], hr.at[0], at_z(c)).start()

    ne[z] = me[z]
    to_z = remote(me.at[pl.ds(0, NZ - 1)], ne.at[pl.ds(0, NZ - 1)], hs.at[0], hr.at[0], at_z(1))

    @pl.loop(0, 4)
    def _(r):
        back[block(r), :] = dot(adj_t[block(r), :], agrad[...])

    to_z.wait_recv()
    scale = 1.0 / (2.0 * NODES * PEERS) ** 0.5
    pz[z] = (sum(ne[q].astype(f32) for q in range(NZ)) * scale).astype(bf16)

    @pl.loop(1, NZ)
    def _(c):
        remote(pz.at[z], pz.at[z], hs.at[1], hr.at[1], at_z(c)).start()

    from_z = remote(me.at[pl.ds(0, NZ - 1)], pz.at[pl.ds(0, NZ - 1)], hs.at[1], hr.at[1], at_z(1))

    def scatter_in(cy):
        source, rows = second.arrived(cy)

        @pl.loop(0, 4)
        def _(r):
            back[block(r), :] += dot(sel[block(r), block(source)], rows)

    scatter_in(ORDER[0])
    from_z.wait_recv()
    for q in range(5):
        pf[v, spot, q * 16 : (q + 1) * 16, :] = pz[q]
    tiny_ref[...] = pz[5].astype(f32)

    @pl.loop(1, 16)
    def _(c):
        remote(pf.at[v, spot], pf.at[v, spot], ps.at[1], pr.at[1], at_plane(c)).start()

    shared = remote(pf.at[v, pl.ds(0, 15)], pf.at[v, pl.ds(0, 15)], ps.at[1], pr.at[1], at_plane(1))
    for cy in ORDER[1:]:
        scatter_in(cy)
    fg_ref[...] = back[...].astype(bf16)
    shared.wait_recv()
    share = remote(pf.at[v], pf.at[v], vs.at[1], vr.at[1], mate)
    share.start()
    remote(pf.at[v], pf.at[1 - v], vs.at[1], vr.at[1], mate).wait_recv()

    swap.wait_send()
    first.finish()
    second.finish()
    for item in (across, plane, to_z, from_z, shared, share):
        item.wait_send()


def results(fg_in, pf, tiny, fg_ref, ew_ref, eb_ref, iw_ref, ib_ref, ow_ref):
    fg_ref[...] = fg_in[...]

    def rows(i):
        return pf[i * 256 : (i + 1) * 256, :].astype(f32)

    for i in range(2):
        for q in range(2):
            ow_ref[i * 256 : (i + 1) * 256, q * 128 : (q + 1) * 128] = rows(2 * i + q)
            col = i * 256 + q * 128
            iw_ref[:, col : col + 128] = rows(4 + 2 * i + q)
    for q in range(2):
        ew_ref[:, q * 128 : (q + 1) * 128] = rows(8 + q)
        eb_ref[:, q * 128 : (q + 1) * 128] = tiny[q : q + 1, :]
    for q in range(4):
        ib_ref[:, q * 128 : (q + 1) * 128] = tiny[2 + q : 3 + q, :]


def local(
    features, local_adjacency, tile_keep, halo_adjacency, send_rows, send_count, target,
    w_encoder, b_encoder, w_predict_in, b_predict_in, w_predict_out,
):
    vmem = pl.BlockSpec(memory_space=pltpu.VMEM)
    anywhere = pl.BlockSpec(memory_space=pl.ANY)
    dma = pltpu.SemaphoreType.DMA
    v16 = lambda *shape: pltpu.VMEM(shape, bf16)
    v32 = lambda *shape: pltpu.VMEM(shape, f32)
    feature_grad, pf, tiny = pl.pallas_call(
        kernel,
        out_shape=(
            jax.ShapeDtypeStruct((NODES, WIDE), bf16),
            jax.ShapeDtypeStruct((2, 16, PART, 128), bf16),
            jax.ShapeDtypeStruct((TINY, 128), f32),
        ),
        in_specs=[anywhere] * 12,
        out_specs=(vmem,) * 3,
        scratch_shapes=[
            v16(NODES, WIDE), v16(NODES, NODES), pltpu.SMEM((8, 8), i32), v16(NODES, NODES),
            pltpu.VMEM((SLOTS, PEERS), i32), pltpu.VMEM((1, PEERS), i32),
            v16(WIDE, WIDE), v32(1, WIDE), v16(WIDE, 2 * WIDE), v32(1, 2 * WIDE), v16(2 * WIDE, WIDE),
            v16(NODES, WIDE), v16(NODES, NODES), v16(NODES, NODES), v16(NODES, NODES),
            v32(NODES, WIDE), v16(NODES, WIDE), v16(NODES, WIDE), v16(NODES, 2 * WIDE),
            v16(NODES, WIDE), v16(NODES, 2 * WIDE), v16(NODES, WIDE), v16(NODES, WIDE), v32(NODES, WIDE),
        ]
        + [v16(NY, PLANE, 16, 128)] * 4
        + [
            v32(2 * HALF, 128), v16(HALF + TINY, 128), v16(HALF + TINY, 128),
            v16(16, PART + TINY, 128), v16(16, PART + TINY, 128),
            v16(NZ, 16, 128), v16(NZ, 16, 128), v16(NZ, 16, 128),
            dma((11,)), dma((2,)), pltpu.SemaphoreType.REGULAR, pltpu.SemaphoreType.REGULAR,
        ]
        + [dma((NY,))] * 4
        + [dma((2,))] * 6,
        compiler_params=pltpu.CompilerParams(
            collective_id=0, has_side_effects=True, vmem_limit_bytes=60 * 1024 * 1024
        ),
    )(
        features[0], local_adjacency[0], tile_keep[0], halo_adjacency[0],
        jnp.swapaxes(send_rows[0], 0, 1), send_count, target[0],
        w_encoder, b_encoder[None], w_predict_in, b_predict_in[None], w_predict_out,
    )
    feature_grad, enc, enc_bias, into, in_bias, out = pl.pallas_call(
        results,
        out_shape=(
            jax.ShapeDtypeStruct((NODES, WIDE), bf16),
            jax.ShapeDtypeStruct((WIDE, WIDE), f32),
            jax.ShapeDtypeStruct((1, WIDE), f32),
            jax.ShapeDtypeStruct((WIDE, 2 * WIDE), f32),
            jax.ShapeDtypeStruct((1, 2 * WIDE), f32),
            jax.ShapeDtypeStruct((2 * WIDE, WIDE), f32),
        ),
        in_specs=[vmem] * 3,
        out_specs=(vmem,) * 6,
    )(
        feature_grad, pf.reshape(2 * HALF, 128), tiny
    )
    return feature_grad[None], enc, enc_bias[0], into, in_bias[0], out


def solution(mesh):
    split = P("view", "dom", None)
    return jax.shard_map(
        local,
        mesh=mesh,
        in_specs=(split, split, split, split, split, P("view", "dom"), split, P(), P(), P(), P(), P()),
        out_specs=(split, P(), P(), P(), P(), P()),
        check_vma=False,
    )
```

time: 109 us -> 69.2 us (0.63)
  Pallas kernels: 95.5 us -> 68.5 us
  local copies, waits for them, and re-layouts: 12.7 us -> 0 us
    pallas_call x1, Pallas kernels: 19.1 us -> 2.54 us  [local(): pl.pallas_call(results, out_shape=(jax.ShapeDtypeStruct((NODES, WIDE), bf...]
    unnamed x30 -> x0, local copies, waits for them, and re-layouts: 12.7 us -> none
    pallas_call x1, Pallas kernels: 76.4 us -> 65.9 us  [local(): pl.pallas_call(kernel, out_shape=(jax.ShapeDtypeStruct((NODES, WIDE), bf1...]
where the time goes in v3:
time: 69.2 us; the launch traced here: 69.1 us
  Pallas kernels  68.5 us (99%)
    pallas_call x1, Pallas kernels, local(): pl.pallas_call(kernel, out_shape=(jax.ShapeDtypeStruct((NODES, WIDE), bf1...  65.9 us
    pallas_call x1, Pallas kernels, local(): pl.pallas_call(results, out_shape=(jax.ShapeDtypeStruct((NODES, WIDE), bf...  2.54 us

profile of v3, /device:TPU:1, one launch (start us, length us, event | category | flops | bytes accessed | tf_op | source)
XLA Modules:
  0.0 69.1 jit_solution(10119039392243178603)
XLA Ops:
  0.6 65.9 %shard_map.163 = (bf16[1024,256]{1,0:T(8,128)(2,1)}, bf16[2,16,80,128]{3,2,1,0:T(8,128)(2,1)}, f32[16,128]{1,0:T(8,128)}) custom-call(bf16[1024,256]{1,0:T(8,128)(2,1)} %bitcast.17, bf16[1024,1024]{1,0:T(8,128)(2,1)} %bitcast.14, s32[8,8]{1,0:T(8,128)} %bitcast.19, bf16[1024,1024]{1,0:T(8,128)(2,1)} %bitcast.15, s32[8,128]{1,0:T(8,128)} %bitcast.20, ...), custom_call_target="tpu_custom_call" | custom-call | tf_op jit(solution)/shard_map/pallas_call | solution.py:401
  66.6 2.5 %shard_map.164 = (bf16[1024,256]{1,0:T(8,128)(2,1)}, f32[256,256]{1,0:T(8,128)}, f32[1,256]{1,0:T(1,128)}, f32[256,512]{1,0:T(8,128)}, f32[1,512]{1,0:T(1,128)}, /*index=5*/f32[512,256]{1,0:T(8,128)}) custom-call(bf16[1024,256]{1,0:T(8,128)(2,1)} %get-tuple-element.15.fg_in, bf16[2560,128]{1,0:T(8,128)(2,1)} %bitcast.16, f32[16,128]{1,0:T(8,128)} %get-tuple-element.17.tiny), custom_call_target="tpu_custom_call" | custom-call | tf_op jit(solution)/shard_map/pallas_call | solution.py:435

commit v4 on v3

--- a/solution.py
+++ b/solution.py
@@ -11,7 +11,8 @@
 ORDER = (2, 1, 3, 0)
 MESH = pl.DeviceIdType.MESH
 PLANE = NX * NZ
-HALF, PART, TINY = 1280, 80, 16
+HALF, PART, TINY = 1280, 40, 16
+GROUP = 32
 loss_scale = 64.0
 
 
@@ -60,9 +61,9 @@
     other, adj_t, halo_t, sel,
     acc, aggr, emb, hid, pgrad, hgrad, egrad, agrad, back,
     o1, c1, o2, c2,
-    gf, m1, n1, ma, na, me, ne, pz,
-    lsem, tsem, x_in, y_in,
-    es1, er1, es2, er2, vs, vr, ps, pr, hs, hr,
+    gf, m1, n1, ma, na, me, ne,
+    lsem, tsem, z_in,
+    es1, er1, es2, er2, vs, vr, gs, gr, ps, pr, hs, hr,
 ):
     v = lax.axis_index("view")
     d = lax.axis_index("dom")
@@ -86,10 +87,8 @@
 
     barrier = pltpu.get_barrier_semaphore()
     pl.semaphore_signal(barrier, inc=1, device_id=mate, device_id_type=MESH)
-    for c in range(1, NY):
-        pl.semaphore_signal(barrier, inc=1, device_id=at_y(c), device_id_type=MESH)
-    for c in range(1, NX):
-        pl.semaphore_signal(barrier, inc=1, device_id=at_x(c), device_id_type=MESH)
+    for c in range(1, 16):
+        pl.semaphore_signal(barrier, inc=1, device_id=at_plane(c), device_id_type=MESH)
     for c in range(1, NZ):
         pl.semaphore_signal(barrier, inc=1, device_id=at_z(c), device_id_type=MESH)
 
@@ -168,19 +167,16 @@
 
     loads[2].wait()
     outgoing(ORDER[0])
-    pl.semaphore_wait(barrier, NZ + NX + NY - 2)
-    for c in range(1, NX):
-        pl.semaphore_signal(x_in, inc=1, device_id=at_x(c), device_id_type=MESH)
+    pl.semaphore_wait(barrier, NZ + 15)
+    for c in range(1, NZ):
+        pl.semaphore_signal(z_in, inc=1, device_id=at_z(c), device_id_type=MESH)
     outgoing(ORDER[1])
-    pl.semaphore_wait(x_in, NX - 1)
-    for c in range(1, NY):
-        pl.semaphore_signal(y_in, inc=1, device_id=at_y(c), device_id_type=MESH)
-    outgoing(ORDER[2])
-    pl.semaphore_wait(y_in, NY - 1)
-    for cy in ORDER[:3]:
+    pl.semaphore_wait(z_in, NZ - 1)
+    for cy in ORDER[:2]:
         first.start(cy)
-    outgoing(ORDER[3])
-    first.start(ORDER[3])
+    for cy in ORDER[2:]:
+        outgoing(cy)
+        first.start(cy)
     swap = remote(target_hbm, other, tsem.at[0], tsem.at[1], mate)
     swap.start()
 
@@ -234,9 +230,9 @@
     for cy in ORDER:
         gather_in(cy)
 
-    @pl.loop(0, 4)
+    @pl.loop(0, 2)
     def _(r):
-        at = block(r)
+        at = block(r, 512)
         agg = acc[at, :].astype(bf16)
         aggr[at, :] = agg
         value, enc_slope = gelu_both(dot(agg, we_ref[...]) + be_ref[...])
@@ -261,82 +257,93 @@
         egrad[at, :] = eg
         agrad[at, :] = dot(eg, we_ref[...], 1, 1).astype(bf16)
 
-    pairs = (
-        (hid, 0, pgrad, 0), (hid, 1, pgrad, 0), (emb, 0, hgrad, 0), (emb, 0, hgrad, 1), (aggr, 0, egrad, 0),
-    )
-    for i, (left, lq, right, rq) in enumerate(pairs):
-        grad = dot(
-            left[:, lq * 256 : (lq + 1) * 256], right[:, rq * 256 : (rq + 1) * 256], 0, 0
-        )
-        gf[i * 512 : i * 512 + 256, :] = grad[:, :128]
-        gf[i * 512 + 256 : (i + 1) * 512, :] = grad[:, 128:]
-    enc_bias = jnp.sum(egrad[...].astype(f32), axis=0, keepdims=True)
-    in_bias = jnp.sum(hgrad[...].astype(f32), axis=0, keepdims=True)
-    bias = jnp.concatenate(
-        [enc_bias[:, :128], enc_bias[:, 128:]]
-        + [in_bias[:, q * 128 : (q + 1) * 128] for q in range(4)]
-        + [jnp.zeros((10, 128), f32)],
-        axis=0,
-    )
-    m1[:HALF, :] = gf[block(1 - v, HALF), :].astype(bf16)
-    m1[HALF:, :] = bias.astype(bf16)
-    across = remote(m1, n1, vs.at[0], vr.at[0], mate)
-    across.start()
-
     def return_rows(cy):
         there = (y + cy) % NY
         o2[cy] = pack(dot(halo_t[block(there), :], agrad[...]))
         second.start(cy)
 
+    def half_of(view):
+        return (
+            lambda: dot(hid[:, block(view)], pgrad[...], 0, 0),
+            lambda: dot(emb[...], hgrad[:, block(view)], 0, 0),
+            lambda: dot(aggr[:, block(view, 128)], egrad[...], 0, 0),
+        )
+
+    def column_sums(ref):
+        return jnp.sum(ref[...].astype(f32), axis=0, keepdims=True)
+
+    cuts = ((0, 512), (512, 512), (1024, 256 + TINY))
+
+    def across(i):
+        part = pl.ds(*cuts[i])
+        return remote(m1.at[part], n1.at[part], vs.at[i], vr.at[i], mate)
+
+    for i, grad in enumerate(half_of(1 - v)):
+        value = grad().astype(bf16)
+        at, n = cuts[i][0], value.shape[0]
+        m1[at : at + n, :] = value[:, :128]
+        m1[at + n : at + 2 * n, :] = value[:, 128:]
+        if i == 2:
+            enc_bias, in_bias = column_sums(egrad), column_sums(hgrad)
+            bias = jnp.concatenate(
+                [enc_bias[:, :128], enc_bias[:, 128:]]
+                + [in_bias[:, q * 128 : (q + 1) * 128] for q in range(4)]
+                + [jnp.zeros((10, 128), f32)],
+                axis=0,
+            )
+            m1[HALF:, :] = bias.astype(bf16)
+        across(i).start()
+    for i, grad in enumerate(half_of(v)):
+        value = grad()
+        at, n = cuts[i][0], value.shape[0]
+        gf[at : at + n, :] = value[:, :128]
+        gf[at + n : at + 2 * n, :] = value[:, 128:]
+
     return_rows(ORDER[0])
     return_rows(ORDER[1])
-
-    spot = d // NZ
-    across.wait_recv()
-    bias = (m1[HALF:, :].astype(f32) + n1[HALF:, :].astype(f32)).astype(bf16)
-
-    @pl.loop(0, 16)
+    pair = z % 2
+    spot = d // NZ * 2 + pair
+
+    def at_group(q):
+        return (v, q // 2 * NZ + (z - pair) + q % 2)
+
+    for i in range(3):
+        across(i).wait_recv()
+    bias = m1[HALF:, :].astype(f32) + n1[HALF:, :].astype(f32)
+    gf[...] += n1[:HALF, :].astype(f32)
+
+    @pl.loop(0, GROUP)
     def _(q):
-        own = gf[pl.ds(v * HALF + q * PART, PART), :] + n1[pl.ds(q * PART, PART), :].astype(f32)
-        ma[q, :PART, :] = own.astype(bf16)
-        ma[q, PART:, :] = bias
-
-    @pl.loop(1, 16)
+        own = gf[pl.ds(pl.multiple_of(q * PART, 8), PART), :]
+        ma[q] = jnp.concatenate([own, bias[:8, :]], axis=0).astype(bf16)
+
+    @pl.loop(1, GROUP)
     def _(c):
-        remote(ma.at[(spot + c) % 16], na.at[spot], ps.at[0], pr.at[0], at_plane(c)).start()
+        q = (spot + c) % GROUP
+        remote(ma.at[q], na.at[spot], ps.at[0], pr.at[0], at_group(q)).start()
 
     na[spot] = ma[spot]
-    plane = remote(ma.at[pl.ds(0, 15)], na.at[pl.ds(0, 15)], ps.at[0], pr.at[0], at_plane(1))
+    others = pl.ds(0, GROUP - 1)
+    group = remote(ma.at[others], na.at[others], ps.at[0], pr.at[0], at_group((spot + 1) % GROUP))
 
     return_rows(ORDER[2])
     return_rows(ORDER[3])
-
-    plane.wait_recv()
-    total = sum(na[q].astype(f32) for q in range(16)).astype(bf16)
-    for q in range(6):
-        me[q] = total[q * 16 : (q + 1) * 16, :]
-    me[6:] = jnp.zeros((2, 16, 128), bf16)
-
-    @pl.loop(1, NZ)
-    def _(c):
-        remote(me.at[(z + c) % NZ], ne.at[z], hs.at[0], hr.at[0], at_z(c)).start()
-
-    ne[z] = me[z]
-    to_z = remote(me.at[pl.ds(0, NZ - 1)], ne.at[pl.ds(0, NZ - 1)], hs.at[0], hr.at[0], at_z(1))
 
     @pl.loop(0, 4)
     def _(r):
         back[block(r), :] = dot(adj_t[block(r), :], agrad[...])
 
-    to_z.wait_recv()
-    scale = 1.0 / (2.0 * NODES * PEERS) ** 0.5
-    pz[z] = (sum(ne[q].astype(f32) for q in range(NZ)) * scale).astype(bf16)
-
-    @pl.loop(1, NZ)
+    group.wait_recv()
+
+    me[...] = sum(na[q].astype(f32) for q in range(GROUP)).astype(bf16)
+    quarter = z // 2
+
+    @pl.loop(1, 4)
     def _(c):
-        remote(pz.at[z], pz.at[z], hs.at[1], hr.at[1], at_z(c)).start()
-
-    from_z = remote(me.at[pl.ds(0, NZ - 1)], pz.at[pl.ds(0, NZ - 1)], hs.at[1], hr.at[1], at_z(1))
+        remote(me, ne.at[quarter], hs.at[0], hr.at[0], at_z(2 * c)).start()
+
+    ne[quarter] = me[...]
+    threes = remote(na.at[pl.ds(0, 3)], ne.at[pl.ds(0, 3)], hs.at[0], hr.at[0], at_z(2))
 
     def scatter_in(cy):
         source, rows = second.arrived(cy)
@@ -346,44 +353,66 @@
             back[block(r), :] += dot(sel[block(r), block(source)], rows)
 
     scatter_in(ORDER[0])
-    from_z.wait_recv()
-    for q in range(5):
-        pf[v, spot, q * 16 : (q + 1) * 16, :] = pz[q]
-    tiny_ref[...] = pz[5].astype(f32)
-
-    @pl.loop(1, 16)
-    def _(c):
-        remote(pf.at[v, spot], pf.at[v, spot], ps.at[1], pr.at[1], at_plane(c)).start()
-
-    shared = remote(pf.at[v, pl.ds(0, 15)], pf.at[v, pl.ds(0, 15)], ps.at[1], pr.at[1], at_plane(1))
+    threes.wait_recv()
+    scale = 1.0 / (2.0 * NODES * PEERS) ** 0.5
+    total = sum(ne[q].astype(f32) for q in range(4)) * scale
+    pf[v, spot] = total.astype(bf16)
+    tiny_ref[...] = total[PART:, :]
+
+    row = 2 * NX
+
+    def share(cy, i):
+        q = (y + cy) % NY * row + (spot + i) % row
+        return remote(pf.at[v, spot], pf.at[v, spot], gs.at[cy], gr.at[cy], at_group(q))
+
+    def shared(cy):
+        part = pl.ds((y - cy + NY) % NY * row, row if cy else row - 1)
+        return remote(pf.at[v, part], pf.at[v, part], gs.at[cy], gr.at[cy], at_y(cy or 1))
+
+    def passed(cy, view):
+        part = pl.ds((y - cy + NY) % NY * row, row)
+        return remote(pf.at[v, part], pf.at[view, part], vs.at[3 + cy], vr.at[3 + cy], mate)
+
+    for cy in ORDER:
+        for i in range(0 if cy else 1, row):
+            share(cy, i).start()
     for cy in ORDER[1:]:
         scatter_in(cy)
     fg_ref[...] = back[...].astype(bf16)
-    shared.wait_recv()
-    share = remote(pf.at[v], pf.at[v], vs.at[1], vr.at[1], mate)
-    share.start()
-    remote(pf.at[v], pf.at[1 - v], vs.at[1], vr.at[1], mate).wait_recv()
+    for cy in (1, 3, 0, 2):
+        shared(cy).wait_recv()
+        passed(cy, v).start()
+    for cy in range(NY):
+        passed(cy, 1 - v).wait_recv()
 
     swap.wait_send()
     first.finish()
     second.finish()
-    for item in (across, plane, to_z, from_z, shared, share):
+    for item in (group, threes):
         item.wait_send()
+    for i in range(3):
+        across(i).wait_send()
+    for cy in range(NY):
+        shared(cy).wait_send()
+        passed(cy, v).wait_send()
 
 
 def results(fg_in, pf, tiny, fg_ref, ew_ref, eb_ref, iw_ref, ib_ref, ow_ref):
     fg_ref[...] = fg_in[...]
 
-    def rows(i):
-        return pf[i * 256 : (i + 1) * 256, :].astype(f32)
-
     for i in range(2):
-        for q in range(2):
-            ow_ref[i * 256 : (i + 1) * 256, q * 128 : (q + 1) * 128] = rows(2 * i + q)
-            col = i * 256 + q * 128
-            iw_ref[:, col : col + 128] = rows(4 + 2 * i + q)
+        lanes = [slice(q * 128, (q + 1) * 128) for q in range(4)]
+        homes = [(ow_ref, i * 256, lanes[q], q * 256, 256) for q in range(2)]
+        homes += [(iw_ref, 0, lanes[2 * i + q], 512 + q * 256, 256) for q in range(2)]
+        homes += [(ew_ref, i * 128, lanes[q], 1024 + q * 128, 128) for q in range(2)]
+        for q in range(GROUP):
+            part = pf[i * GROUP + q].astype(f32)
+            low = q * PART
+            for ref, top, lane, first, count in homes:
+                begin, end = max(low, first), min(low + PART, first + count)
+                if begin < end:
+                    ref[top + begin - first : top + end - first, lane] = part[begin - low : end - low, :]
     for q in range(2):
-        ew_ref[:, q * 128 : (q + 1) * 128] = rows(8 + q)
         eb_ref[:, q * 128 : (q + 1) * 128] = tiny[q : q + 1, :]
     for q in range(4):
         ib_ref[:, q * 128 : (q + 1) * 128] = tiny[2 + q : 3 + q, :]
@@ -402,8 +431,8 @@
         kernel,
         out_shape=(
             jax.ShapeDtypeStruct((NODES, WIDE), bf16),
-            jax.ShapeDtypeStruct((2, 16, PART, 128), bf16),
-            jax.ShapeDtypeStruct((TINY, 128), f32),
+            jax.ShapeDtypeStruct((2, GROUP, PART + 8, 128), bf16),
+            jax.ShapeDtypeStruct((8, 128), f32),
         ),
         in_specs=[anywhere] * 12,
         out_specs=(vmem,) * 3,
@@ -417,13 +446,12 @@
         ]
         + [v16(NY, PLANE, 16, 128)] * 4
         + [
-            v32(2 * HALF, 128), v16(HALF + TINY, 128), v16(HALF + TINY, 128),
-            v16(16, PART + TINY, 128), v16(16, PART + TINY, 128),
-            v16(NZ, 16, 128), v16(NZ, 16, 128), v16(NZ, 16, 128),
-            dma((11,)), dma((2,)), pltpu.SemaphoreType.REGULAR, pltpu.SemaphoreType.REGULAR,
+            v32(HALF, 128), v16(HALF + TINY, 128), v16(HALF + TINY, 128),
+            v16(GROUP, PART + 8, 128), v16(GROUP, PART + 8, 128), v16(PART + 8, 128), v16(4, PART + 8, 128),
+            dma((11,)), dma((2,)), pltpu.SemaphoreType.REGULAR,
         ]
         + [dma((NY,))] * 4
-        + [dma((2,))] * 6,
+        + [dma((7,))] * 2 + [dma((NY,))] * 2 + [dma((1,))] * 4,
         compiler_params=pltpu.CompilerParams(
             collective_id=0, has_side_effects=True, vmem_limit_bytes=60 * 1024 * 1024
         ),
@@ -445,7 +473,7 @@
         in_specs=[vmem] * 3,
         out_specs=(vmem,) * 6,
     )(
-        feature_grad, pf.reshape(2 * HALF, 128), tiny
+        feature_grad, pf.reshape(2 * GROUP, PART + 8, 128), tiny
     )
     return feature_grad[None], enc, enc_bias[0], into, in_bias[0], out
 

time: 69.2 us -> 67.1 us (0.970)
  Pallas kernels: 68.5 us -> 66.3 us
    pallas_call x1, Pallas kernels: 65.9 us -> 63.7 us  [local(): pl.pallas_call(kernel, out_shape=(jax.ShapeDtypeStruct((NODES, WIDE), bf1...]
where the time goes in v4:
time: 67.1 us; the launch traced here: 67 us
  Pallas kernels  66.3 us (99%)
    pallas_call x1, Pallas kernels, local(): pl.pallas_call(kernel, out_shape=(jax.ShapeDtypeStruct((NODES, WIDE), bf1...  63.7 us
    pallas_call x1, Pallas kernels, local(): pl.pallas_call(results, out_shape=(jax.ShapeDtypeStruct((NODES, WIDE), bf...  2.6 us

profile of v4, /device:TPU:1, one launch (start us, length us, event | category | flops | bytes accessed | tf_op | source)
XLA Modules:
  0.0 67.0 jit_solution(2073493515399532834)
XLA Ops:
  0.6 63.7 %shard_map.163 = (bf16[1024,256]{1,0:T(8,128)(2,1)}, bf16[2,32,48,128]{3,2,1,0:T(8,128)(2,1)}, f32[8,128]{1,0:T(8,128)}) custom-call(bf16[1024,256]{1,0:T(8,128)(2,1)} %bitcast.17, bf16[1024,1024]{1,0:T(8,128)(2,1)} %bitcast.14, s32[8,8]{1,0:T(8,128)} %bitcast.19, bf16[1024,1024]{1,0:T(8,128)(2,1)} %bitcast.15, s32[8,128]{1,0:T(8,128)} %bitcast.20, ...), custom_call_target="tpu_custom_call" | custom-call | tf_op jit(solution)/shard_map/pallas_call | solution.py:430
  64.4 2.6 %shard_map.164 = (bf16[1024,256]{1,0:T(8,128)(2,1)}, f32[256,256]{1,0:T(8,128)}, f32[1,256]{1,0:T(1,128)}, f32[256,512]{1,0:T(8,128)}, f32[1,512]{1,0:T(1,128)}, /*index=5*/f32[512,256]{1,0:T(8,128)}) custom-call(bf16[1024,256]{1,0:T(8,128)(2,1)} %get-tuple-element.15.fg_in, bf16[64,48,128]{2,1,0:T(8,128)(2,1)} %bitcast.16, f32[8,128]{1,0:T(8,128)} %get-tuple-element.17.tiny), custom_call_target="tpu_custom_call" | custom-call | tf_op jit(solution)/shard_map/pallas_call | solution.py:463

commit v5 on v4

--- a/solution.py
+++ b/solution.py
@@ -220,9 +220,7 @@
     def gather_in(cy):
         source, rows = first.arrived(cy)
 
-        @pl.loop(0, 4)
-        def _(r):
-            acc[block(r), :] += dot(halo[block(r), block(source)], rows)
+        acc[...] += dot(halo[:, block(source)], rows)
 
     for item in loads[6:]:
         item.wait()
@@ -230,9 +228,9 @@
     for cy in ORDER:
         gather_in(cy)
 
-    @pl.loop(0, 2)
+    @pl.loop(0, 1)
     def _(r):
-        at = block(r, 512)
+        at = block(r, NODES)
         agg = acc[at, :].astype(bf16)
         aggr[at, :] = agg
         value, enc_slope = gelu_both(dot(agg, we_ref[...]) + be_ref[...])
@@ -300,7 +298,6 @@
         gf[at + n : at + 2 * n, :] = value[:, 128:]
 
     return_rows(ORDER[0])
-    return_rows(ORDER[1])
     pair = z % 2
     spot = d // NZ * 2 + pair
 
@@ -312,22 +309,22 @@
     bias = m1[HALF:, :].astype(f32) + n1[HALF:, :].astype(f32)
     gf[...] += n1[:HALF, :].astype(f32)
 
-    @pl.loop(0, GROUP)
-    def _(q):
+    def part(q):
         own = gf[pl.ds(pl.multiple_of(q * PART, 8), PART), :]
-        ma[q] = jnp.concatenate([own, bias[:8, :]], axis=0).astype(bf16)
+        return jnp.concatenate([own, bias[:8, :]], axis=0).astype(bf16)
 
     @pl.loop(1, GROUP)
     def _(c):
         q = (spot + c) % GROUP
+        ma[q] = part(q)
         remote(ma.at[q], na.at[spot], ps.at[0], pr.at[0], at_group(q)).start()
 
-    na[spot] = ma[spot]
+    na[spot] = part(spot)
     others = pl.ds(0, GROUP - 1)
     group = remote(ma.at[others], na.at[others], ps.at[0], pr.at[0], at_group((spot + 1) % GROUP))
 
+    return_rows(ORDER[1])
     return_rows(ORDER[2])
-    return_rows(ORDER[3])
 
     @pl.loop(0, 4)
     def _(r):
@@ -344,13 +341,12 @@
 
     ne[quarter] = me[...]
     threes = remote(na.at[pl.ds(0, 3)], ne.at[pl.ds(0, 3)], hs.at[0], hr.at[0], at_z(2))
+    return_rows(ORDER[3])
 
     def scatter_in(cy):
         source, rows = second.arrived(cy)
 
-        @pl.loop(0, 4)
-        def _(r):
-            back[block(r), :] += dot(sel[block(r), block(source)], rows)
+        back[...] += dot(sel[:, block(source)], rows)
 
     scatter_in(ORDER[0])
     threes.wait_recv()

time: 67.1 us -> 64.2 us (0.957)
  Pallas kernels: 66.3 us -> 63.5 us
    pallas_call x1, Pallas kernels: 63.7 us -> 60.9 us  [local(): pl.pallas_call(kernel, out_shape=(jax.ShapeDtypeStruct((NODES, WIDE), bf1...]
where the time goes in v5:
time: 64.2 us; the launch traced here: 64.1 us
  Pallas kernels  63.5 us (99%)
    pallas_call x1, Pallas kernels, local(): pl.pallas_call(kernel, out_shape=(jax.ShapeDtypeStruct((NODES, WIDE), bf1...  60.9 us
    pallas_call x1, Pallas kernels, local(): pl.pallas_call(results, out_shape=(jax.ShapeDtypeStruct((NODES, WIDE), bf...  2.6 us

profile of v5, /device:TPU:1, one launch (start us, length us, event | category | flops | bytes accessed | tf_op | source)
XLA Modules:
  0.0 64.1 jit_solution(10328362068907763753)
XLA Ops:
  0.6 60.9 %shard_map.163 = (bf16[1024,256]{1,0:T(8,128)(2,1)}, bf16[2,32,48,128]{3,2,1,0:T(8,128)(2,1)}, f32[8,128]{1,0:T(8,128)}) custom-call(bf16[1024,256]{1,0:T(8,128)(2,1)} %bitcast.17, bf16[1024,1024]{1,0:T(8,128)(2,1)} %bitcast.14, s32[8,8]{1,0:T(8,128)} %bitcast.19, bf16[1024,1024]{1,0:T(8,128)(2,1)} %bitcast.15, s32[8,128]{1,0:T(8,128)} %bitcast.20, ...), custom_call_target="tpu_custom_call" | custom-call | tf_op jit(solution)/shard_map/pallas_call | solution.py:426
  61.5 2.6 %shard_map.164 = (bf16[1024,256]{1,0:T(8,128)(2,1)}, f32[256,256]{1,0:T(8,128)}, f32[1,256]{1,0:T(1,128)}, f32[256,512]{1,0:T(8,128)}, f32[1,512]{1,0:T(1,128)}, /*index=5*/f32[512,256]{1,0:T(8,128)}) custom-call(bf16[1024,256]{1,0:T(8,128)(2,1)} %get-tuple-element.15.fg_in, bf16[64,48,128]{2,1,0:T(8,128)(2,1)} %bitcast.16, f32[8,128]{1,0:T(8,128)} %get-tuple-element.17.tiny), custom_call_target="tpu_custom_call" | custom-call | tf_op jit(solution)/shard_map/pallas_call | solution.py:459

commit v6 on v5

--- a/solution.py
+++ b/solution.py
@@ -205,18 +205,6 @@
                 ].T
 
     transpose(halo, halo_t)
-    transpose(adj, adj_t)
-
-    spread = jnp.where(iota((PEERS, NODES), 1) // 8 == iota((PEERS, NODES), 0), 1.0, 0.0).astype(bf16)
-    parts = dot(code, spread)
-    slot = iota((16, NODES), 0)
-    weight = jnp.where((slot & 7) == (iota((16, NODES), 1) & 7), jnp.where(slot < 8, 32.0, 1.0), 0.0)
-    row = jnp.sum(parts * weight, axis=0, keepdims=True).astype(i32)
-
-    @pl.loop(0, 4)
-    def _(r):
-        sel[block(r), :] = jnp.where(iota((256, NODES), 0) + r * 256 == row, 1.0, 0.0).astype(bf16)
-
     def gather_in(cy):
         source, rows = first.arrived(cy)
 
@@ -297,7 +285,7 @@
         gf[at : at + n, :] = value[:, :128]
         gf[at + n : at + 2 * n, :] = value[:, 128:]
 
-    return_rows(ORDER[0])
+    return_rows(0)
     pair = z % 2
     spot = d // NZ * 2 + pair
 
@@ -323,8 +311,20 @@
     others = pl.ds(0, GROUP - 1)
     group = remote(ma.at[others], na.at[others], ps.at[0], pr.at[0], at_group((spot + 1) % GROUP))
 
-    return_rows(ORDER[1])
-    return_rows(ORDER[2])
+    return_rows(3)
+    return_rows(1)
+
+    transpose(adj, adj_t)
+
+    spread = jnp.where(iota((PEERS, NODES), 1) // 8 == iota((PEERS, NODES), 0), 1.0, 0.0).astype(bf16)
+    parts = dot(code, spread)
+    slot = iota((16, NODES), 0)
+    weight = jnp.where((slot & 7) == (iota((16, NODES), 1) & 7), jnp.where(slot < 8, 32.0, 1.0), 0.0)
+    row = jnp.sum(parts * weight, axis=0, keepdims=True).astype(i32)
+
+    @pl.loop(0, 4)
+    def _(r):
+        sel[block(r), :] = jnp.where(iota((256, NODES), 0) + r * 256 == row, 1.0, 0.0).astype(bf16)
 
     @pl.loop(0, 4)
     def _(r):
@@ -341,14 +341,14 @@
 
     ne[quarter] = me[...]
     threes = remote(na.at[pl.ds(0, 3)], ne.at[pl.ds(0, 3)], hs.at[0], hr.at[0], at_z(2))
-    return_rows(ORDER[3])
+    return_rows(2)
 
     def scatter_in(cy):
         source, rows = second.arrived(cy)
 
         back[...] += dot(sel[:, block(source)], rows)
 
-    scatter_in(ORDER[0])
+    scatter_in(0)
     threes.wait_recv()
     scale = 1.0 / (2.0 * NODES * PEERS) ** 0.5
     total = sum(ne[q].astype(f32) for q in range(4)) * scale
@@ -372,7 +372,7 @@
     for cy in ORDER:
         for i in range(0 if cy else 1, row):
             share(cy, i).start()
-    for cy in ORDER[1:]:
+    for cy in (3, 1, 2):
         scatter_in(cy)
     fg_ref[...] = back[...].astype(bf16)
     for cy in (1, 3, 0, 2):

time: 64.2 us -> 64.3 us (level)
  no operation moved by 1% of the time
where the time goes in v6:
time: 64.3 us; the launch traced here: 64.1 us
  Pallas kernels  63.5 us (99%)
    pallas_call x1, Pallas kernels, local(): pl.pallas_call(kernel, out_shape=(jax.ShapeDtypeStruct((NODES, WIDE), bf1...  60.9 us
    pallas_call x1, Pallas kernels, local(): pl.pallas_call(results, out_shape=(jax.ShapeDtypeStruct((NODES, WIDE), bf...  2.6 us

profile of v6, /device:TPU:1, one launch (start us, length us, event | category | flops | bytes accessed | tf_op | source)
XLA Modules:
  0.0 64.1 jit_solution(4784095802060356767)
XLA Ops:
  0.6 60.9 %shard_map.163 = (bf16[1024,256]{1,0:T(8,128)(2,1)}, bf16[2,32,48,128]{3,2,1,0:T(8,128)(2,1)}, f32[8,128]{1,0:T(8,128)}) custom-call(bf16[1024,256]{1,0:T(8,128)(2,1)} %bitcast.17, bf16[1024,1024]{1,0:T(8,128)(2,1)} %bitcast.14, s32[8,8]{1,0:T(8,128)} %bitcast.19, bf16[1024,1024]{1,0:T(8,128)(2,1)} %bitcast.15, s32[8,128]{1,0:T(8,128)} %bitcast.20, ...), custom_call_target="tpu_custom_call" | custom-call | tf_op jit(solution)/shard_map/pallas_call | solution.py:426
  61.5 2.6 %shard_map.164 = (bf16[1024,256]{1,0:T(8,128)(2,1)}, f32[256,256]{1,0:T(8,128)}, f32[1,256]{1,0:T(1,128)}, f32[256,512]{1,0:T(8,128)}, f32[1,512]{1,0:T(1,128)}, /*index=5*/f32[512,256]{1,0:T(8,128)}) custom-call(bf16[1024,256]{1,0:T(8,128)(2,1)} %get-tuple-element.15.fg_in, bf16[64,48,128]{2,1,0:T(8,128)(2,1)} %bitcast.16, f32[8,128]{1,0:T(8,128)} %get-tuple-element.17.tiny), custom_call_target="tpu_custom_call" | custom-call | tf_op jit(solution)/shard_map/pallas_call | solution.py:459
